TPU v7x, 512 devices: a whole 4x4x16 slice. The times are simulated.
512 devices in a mesh: row: 32 (over y, x, core), col: 16 (over z).
Axes of the slice: x: 4, y: 4, z: 16, core: 2. Of those that a mesh axis runs over, the one named last changes fastest.
Arguments:
- matrix: float32 [12288, 12288], P('row', 'col'), may hold values from -10 to 10, as said below
- panel: float32 [12288, 64], P('row'), may hold values from -1.12763724 to 1.12763724
Outputs:
- updated: float32 [12288, 12288], P('row', 'col')
- band_block: float32 [64, 64], replicated
Inputs may be any that keep to these rules, and one draw needn't show every extreme that they name: matrix is exactly symmetric.
All inputs are finite; a program needn't handle non-finite values.
Results may differ from a plain program's by a relative error of at most 0.0002.
Values sent between devices are 32-bit elements; how exact they have to be, the bound alone decides.
A program may use at most 64 MiB of HBM per device.

v0:
```python
import jax
import jax.numpy as jnp
from jax import lax
from jax.sharding import PartitionSpec as P

precise = lax.Precision.HIGHEST


def partner_2(block, axis, stride):
    count = lax.axis_size(axis)
    route = []
    for low in range(count):
        high = low | 1 << stride
        if high != low and high < count:
            route += [(low, high), (high, low)]
    return lax.ppermute(block, axis, route)


def from_root(value, axis, source):
    kept = jnp.where(lax.axis_index(axis) == source, value, 0).astype(value.dtype)
    return lax.psum(kept, axis)


def upper_cholesky(gram_block):
    order_now = gram_block.shape[0]
    positions = jnp.arange(order_now)

    def one_column(column_index, lower_part):
        gram_column = lax.dynamic_slice_in_dim(gram_block, column_index, 1, 1)[:, 0]
        lower_row = lax.dynamic_slice_in_dim(lower_part, column_index, 1, 0)[0]
        earlier = jnp.where(positions < column_index, lower_row, 0.0)
        reduced = gram_column - jnp.dot(lower_part, earlier, precision=precise)
        pivot_value = jnp.sum(jnp.where(positions == column_index, reduced, 0.0))
        diagonal_value = jnp.sqrt(pivot_value)
        new_column = jnp.where(positions > column_index, reduced / diagonal_value, 0.0) + jnp.where(
            positions == column_index, diagonal_value, 0.0
        )
        return jnp.where(positions[None, :] == column_index, new_column[:, None], lower_part)

    lower_part = lax.fori_loop(
        0, order_now, one_column, jnp.zeros((order_now, order_now), jnp.float32)
    )
    return lower_part.T


def upper_inverse(upper_block):
    order_now = upper_block.shape[0]
    positions = jnp.arange(order_now)

    def one_row(step_count, inverse_part):
        row_at = order_now - 1 - step_count
        upper_row = lax.dynamic_slice_in_dim(upper_block, row_at, 1, 0)[0]
        diagonal_value = jnp.sum(jnp.where(positions == row_at, upper_row, 0.0))
        beyond = jnp.where(positions > row_at, upper_row, 0.0)
        unit_row = jnp.where(positions == row_at, 1.0, 0.0)
        new_row = (unit_row - jnp.dot(beyond, inverse_part, precision=precise)) / diagonal_value
        return jnp.where(positions[:, None] == row_at, new_row[None, :], inverse_part)

    return lax.fori_loop(0, order_now, one_row, jnp.zeros((order_now, order_now), jnp.float32))


def small_factor(block_in):
    order_now = block_in.shape[0]
    positions = jnp.arange(order_now)

    def one_pivot(pivot_index, state_pair):
        working, lower_whole = state_pair
        pivot_column = lax.dynamic_slice_in_dim(working, pivot_index, 1, 1)[:, 0]
        pivot_row = lax.dynamic_slice_in_dim(working, pivot_index, 1, 0)[0]
        pivot_value = jnp.sum(jnp.where(positions == pivot_index, pivot_column, 0.0))
        multipliers = jnp.where(positions > pivot_index, pivot_column / pivot_value, 0.0)
        lower_whole = lower_whole + multipliers[:, None] * (
            positions[None, :] == pivot_index
        ).astype(jnp.float32)
        working = working - multipliers[:, None] * pivot_row[None, :]
        return (working, lower_whole)

    working, lower_whole = lax.fori_loop(
        0, order_now, one_pivot, (block_in, jnp.eye(order_now, dtype=jnp.float32))
    )
    return (lower_whole, jnp.triu(working))


def body(matrix, panel):
    local_rows, local_columns = matrix.shape
    panel_width = panel.shape[1]
    row_index = lax.axis_index("row")
    current_column_index = lax.axis_index("col")
    local_inner = jnp.dot(panel.T, panel, precision=precise)
    head_rows = panel[:panel_width]
    band_factor = -upper_cholesky(local_inner)
    levels = lax.axis_size("row").bit_length() - 1
    for bit_level in range(levels):
        partner = partner_2(band_factor, "row", bit_level)
        keeps_first = row_index >> bit_level & 1 == 0
        earlier_one = jnp.where(keeps_first, band_factor, partner)
        later_one = jnp.where(keeps_first, partner, band_factor)
        paired = jnp.dot(earlier_one.T, earlier_one, precision=precise) + jnp.dot(
            later_one.T, later_one, precision=precise
        )
        band_factor = -upper_cholesky(paired)
    head_rows = from_root(head_rows, "row", 0)
    factor_inverse = upper_inverse(band_factor)
    orthogonal_rows = jnp.dot(panel, factor_inverse, precision=precise)
    orthogonal_head = jnp.dot(head_rows, factor_inverse, precision=precise)
    identity = jnp.eye(panel_width, dtype=jnp.float32)
    lower_whole, upper_whole = small_factor(orthogonal_head - identity)
    global_rows = row_index * local_rows + jnp.arange(local_rows)
    unit_rows = (global_rows[:, None] == jnp.arange(panel_width)[None, :]).astype(jnp.float32)
    reflect_rows = jnp.dot(
        orthogonal_rows - unit_rows, upper_inverse(upper_whole), precision=precise
    )
    triangle = -jnp.dot(upper_whole, upper_inverse(lower_whole.T), precision=precise)
    gathered_reflect = lax.all_gather(reflect_rows, "row", axis=0, tiled=True)
    reflect_columns = lax.dynamic_slice_in_dim(
        gathered_reflect, current_column_index * local_columns, local_columns, 0
    )
    partial_product = lax.dot_general(
        matrix, reflect_rows, (((0,), (0,)), ((), ())), precision=precise
    )
    product = lax.psum(partial_product, "row")
    applied_cols = jnp.dot(product, triangle, precision=precise)
    inner_part = jnp.dot(reflect_columns.T, applied_cols, precision=precise)
    inner_total = lax.psum(inner_part, "col")
    coupling = jnp.dot(triangle.T, inner_total, precision=precise)
    corrected_cols = applied_cols - 0.5 * jnp.dot(reflect_columns, coupling, precision=precise)
    gathered_corrected = lax.all_gather(corrected_cols, "col", axis=0, tiled=True)
    corrected_rows = lax.dynamic_slice_in_dim(
        gathered_corrected, row_index * local_rows, local_rows, 0
    )
    left_factor = jnp.concatenate([reflect_rows, corrected_rows], 1)
    right_factor = jnp.concatenate([corrected_cols, reflect_columns], 1)
    updated = matrix - lax.dot_general(
        left_factor, right_factor, (((1,), (1,)), ((), ())), precision=precise
    )
    return (updated, band_factor)


def solution(mesh):
    return jax.shard_map(
        body,
        mesh=mesh,
        in_specs=(P("row", "col"), P("row", None)),
        out_specs=(P("row", "col"), P()),
        check_vma=False,
    )
```

profile of v0, /device:TPU:1, one launch (start us, length us, event | category | flops | bytes accessed | tf_op | source)
XLA Modules:
  0.0 1392.1 jit_solution(851780001571916975)
XLA Ops:
  7.2 1.2 fusion.154
  8.5 101.3 %while.159 = (s32[]{:T(128)}, f32[64,64]{1,0:T(8,128)S(1)}, f32[64,64]{0,1:T(8,128)S(1)}, s32[]{:T(128)}, s32[]{:T(128)}) while((s32[]{:T(128)}, f32[64,64]{1,0:T(8,128)S(1)}, f32[64,64]{0,1:T(8,128)S(1)}, s32[]{:T(128)}, s32[]{:T(128)}) %tuple.367), condition=%wide.region_2.3_spmd.clone.clone, body=%wide.region_0.2_spmd.clone.clone.sunk | while | flops 62274 | bytes 102632 | solution.py:40
  109.8 8.8 collective-permute-start
  119.9 101.3 %while.160 = (s32[]{:T(128)}, f32[64,64]{1,0:T(8,128)S(1)}, f32[64,64]{0,1:T(8,128)S(1)}, s32[]{:T(128)}, s32[]{:T(128)}) while((s32[]{:T(128)}, f32[64,64]{1,0:T(8,128)S(1)}, f32[64,64]{0,1:T(8,128)S(1)}, s32[]{:T(128)}, s32[]{:T(128)}) %tuple.370), condition=%wide.region_5.6_spmd.clone.clone, body=%wide.region_3.5_spmd.clone.clone.sunk | while | flops 62274 | bytes 102632 | solution.py:40
  221.2 1.9 collective-permute-start.1
  223.2 2.7 collective-permute-done.1
  226.3 101.3 %while.161 = (s32[]{:T(128)}, f32[64,64]{1,0:T(8,128)S(1)}, f32[64,64]{0,1:T(8,128)S(1)}, s32[]{:T(128)}, s32[]{:T(128)}) while((s32[]{:T(128)}, f32[64,64]{1,0:T(8,128)S(1)}, f32[64,64]{0,1:T(8,128)S(1)}, s32[]{:T(128)}, s32[]{:T(128)}) %tuple.373), condition=%wide.region_8.9_spmd.clone.clone, body=%wide.region_6.8_spmd.clone.clone.sunk | while | flops 62274 | bytes 102632 | solution.py:40
  327.7 1.9 collective-permute-start.2
  329.6 4.2 collective-permute-done.2
  334.3 101.3 %while.162 = (s32[]{:T(128)}, f32[64,64]{1,0:T(8,128)S(1)}, f32[64,64]{0,1:T(8,128)S(1)}, s32[]{:T(128)}, s32[]{:T(128)}) while((s32[]{:T(128)}, f32[64,64]{1,0:T(8,128)S(1)}, f32[64,64]{0,1:T(8,128)S(1)}, s32[]{:T(128)}, s32[]{:T(128)}) %tuple.376), condition=%wide.region_11.12_spmd.clone.clone, body=%wide.region_9.11_spmd.clone.clone.sunk | while | flops 62274 | bytes 102632 | solution.py:40
  435.6 1.9 collective-permute-start.3
  437.6 2.7 collective-permute-done.3
  440.7 101.3 %while.163 = (s32[]{:T(128)}, f32[64,64]{1,0:T(8,128)S(1)}, f32[64,64]{0,1:T(8,128)S(1)}, s32[]{:T(128)}, s32[]{:T(128)}) while((s32[]{:T(128)}, f32[64,64]{1,0:T(8,128)S(1)}, f32[64,64]{0,1:T(8,128)S(1)}, s32[]{:T(128)}, s32[]{:T(128)}) %tuple.379), condition=%wide.region_14.15_spmd.clone.clone, body=%wide.region_12.14_spmd.clone.clone.sunk | while | flops 62274 | bytes 102632 | solution.py:40
  542.1 1.9 collective-permute-start.4
  544.1 121.9 %psum.21 = f32[64,64]{1,0:T(8,128)S(1)} all-reduce(f32[64,64]{1,0:T(8,128)S(1)} %broadcast_select_fusion.12), channel_id=1, replica_groups=mesh['row'=32,'col'=16] {'row'}, use_global_device_ids=true, to_apply=%region_21.22 | all-reduce | flops 4096 | bytes 32768 | tf_op jit(solution)/shard_map/psum | solution.py:21
  666.5 102.2 %while.164 = (s32[]{:T(128)}, f32[64,64]{1,0:T(8,128)S(1)}, f32[64,64]{0,1:T(8,128)S(1)}, s32[]{:T(128)}, s32[]{:T(128)}) while((s32[]{:T(128)}, f32[64,64]{1,0:T(8,128)S(1)}, f32[64,64]{0,1:T(8,128)S(1)}, s32[]{:T(128)}, s32[]{:T(128)}) %tuple.382), condition=%wide.region_17.18_spmd.clone.clone, body=%wide.region_15.17_spmd.clone.clone.sunk | while | flops 62274 | bytes 102632 | solution.py:40
  768.8 95.1 %while.165 = (s32[]{:T(128)}, f32[64,64]{1,0:T(8,128)S(1)}, f32[64,64]{1,0:T(8,128)S(1)}, s32[]{:T(128)}, s32[]{:T(128)}, /*index=5*/s32[]{:T(128)}, s32[]{:T(128)}) while((s32[]{:T(128)}, f32[64,64]{1,0:T(8,128)S(1)}, f32[64,64]{1,0:T(8,128)S(1)}, s32[]{:T(128)}, s32[]{:T(128)}, /*index=5*/s32[]{:T(128)}, ...), condition=%wide.region_20.21_spmd.clone.clone, body=%wide.region_18.20_spmd.clone.clone.sunk | while | flops 62086 | bytes 69153 | solution.py:59
  864.2 100.7 %while.158 = (s32[]{:T(128)}, f32[64,64]{0,1:T(8,128)S(1)}, f32[64,64]{0,1:T(8,128)S(1)}, s32[]{:T(128)}) while((s32[]{:T(128)}, f32[64,64]{0,1:T(8,128)S(1)}, f32[64,64]{0,1:T(8,128)S(1)}, s32[]{:T(128)}) %tuple.388), condition=%wide.region_24.25_spmd.clone.clone, body=%wide.region_22.24_spmd.clone.clone.sunk | while | flops 16897 | bytes 69965 | solution.py:78
  965.0 95.1 %while.166 = (s32[]{:T(128)}, f32[64,64]{1,0:T(8,128)S(1)}, f32[64,64]{1,0:T(8,128)S(1)}, s32[]{:T(128)}, s32[]{:T(128)}, /*index=5*/s32[]{:T(128)}, s32[]{:T(128)}) while((s32[]{:T(128)}, f32[64,64]{1,0:T(8,128)S(1)}, f32[64,64]{1,0:T(8,128)S(1)}, s32[]{:T(128)}, s32[]{:T(128)}, /*index=5*/s32[]{:T(128)}, ...), condition=%wide.region_27.28_spmd.clone.clone, body=%wide.region_25.27_spmd.clone.clone.sunk | while | flops 62086 | bytes 69153 | solution.py:59
  1060.7 1.5 convolution_bitcast_fusion.9
  1063.0 103.2 %while.167 = (s32[]{:T(128)}, f32[64,64]{1,0:T(8,128)S(1)}, f32[64,64]{1,0:T(8,128)S(1)}, s32[]{:T(128)}, s32[]{:T(128)}, /*index=5*/s32[]{:T(128)}, s32[]{:T(128)}) while((s32[]{:T(128)}, f32[64,64]{1,0:T(8,128)S(1)}, f32[64,64]{1,0:T(8,128)S(1)}, s32[]{:T(128)}, s32[]{:T(128)}, /*index=5*/s32[]{:T(128)}, ...), condition=%wide.region_31.32_spmd.clone.clone, body=%wide.region_29.31_spmd.clone.clone.sunk | while | flops 62086 | bytes 69153 | solution.py:59
  1063.7 0.8 fusion.236
  1065.4 0.8 fusion.236
  1067.0 0.8 fusion.236
  1068.6 0.8 fusion.236
  1070.2 0.8 fusion.236
  1071.8 0.8 fusion.236
  1073.4 0.8 fusion.236
  1075.0 0.8 fusion.236
  1076.6 0.8 fusion.236
  1078.2 0.8 fusion.236
  1079.9 0.8 fusion.236
  1081.5 0.8 fusion.236
  1083.1 0.8 fusion.236
  1084.7 0.8 fusion.236
  1086.3 0.8 fusion.236
  1092.8 0.8 fusion.236
  1094.4 0.8 fusion.236
  1115.3 0.8 fusion.236
  1116.9 0.8 fusion.236
  1125.0 0.8 fusion.236
  1126.6 0.8 fusion.236
  1128.2 0.8 fusion.236
  1129.8 0.8 fusion.236
  1131.4 0.8 fusion.236
  1133.0 0.8 fusion.236
  1134.7 0.8 fusion.236
  1152.4 0.8 fusion.236
  1155.6 0.8 fusion.236
  1157.2 0.8 fusion.236
  1158.8 0.8 fusion.236
  1160.4 0.8 fusion.236
  1162.1 0.8 fusion.236
  1163.7 0.8 fusion.236
  1165.3 0.8 fusion.236
  1166.4 28.4 %all-reduce.2.cloned.1.call-done = f32[768,64]{0,1:T(8,128)} async-done(((f32[768,64]{0,1:T(8,128)}), f32[768,64]{0,1:T(8,128)}) %all-reduce.2.cloned.1.call-update) | async-done | bytes 196624 | tf_op jit(solution)/shard_map/psum | solution.py:121
  1194.8 1.3 fusion.156
  1196.0 62.8 %all-gather.3.cloned.1.call-done = f32[12288,64]{0,1:T(8,128)} async-done(((f32[384,64]{0,1:T(8,128)}), f32[12288,64]{0,1:T(8,128)}) %all-gather.3.cloned.1.call-update) | async-done | bytes 3145744 | tf_op jit(solution)/shard_map/all_gather | solution.py:114
  1258.9 0.9 constant_dynamic-slice_fusion.8
  1260.2 43.4 %psum.23 = f32[64,64]{1,0:T(8,128)S(1)} all-reduce(f32[64,64]{1,0:T(8,128)S(1)} %fusion.157), channel_id=1, replica_groups=mesh['row'=32,'col'=16] {'col'}, use_global_device_ids=true, to_apply=%region_32.33 | all-reduce | flops 4096 | bytes 32768 | tf_op jit(solution)/shard_map/psum | solution.py:124
  1303.8 1.1 fusion.118
  1304.9 76.7 %all-gather.5.cloned.1.call-done = f32[12288,64]{0,1:T(8,128)} async-done(((f32[768,64]{0,1:T(8,128)}), f32[12288,64]{0,1:T(8,128)}) %all-gather.5.cloned.1.call-update) | async-done | bytes 3145744 | tf_op jit(solution)/shard_map/all_gather | solution.py:127
  1381.6 0.9 constant_dynamic-slice_fusion.7
  1382.5 3.1 convolution_subtract_fusion
  (3040 shorter events, 703.2 us)
Async XLA Ops:
  7.2 111.5 %slice-start = ((f32[384,64]{0,1:T(8,128)}), f32[64,64]{0,1:T(8,128)S(1)}, s32[]{:S(2)}) async-start(f32[384,64]{0,1:T(8,128)} %param.23), calls=%async_computation.3 | async-start | bytes 65536 | tf_op jit(solution)/shard_map/slice | solution.py:90
  7.2 1187.6 %all-reduce.2.cloned.1.call-start = ((), (), s32[]{:S(2)}) async-start(), calls=%async_computation | async-start | bytes 393216 | tf_op jit(solution)/shard_map/psum | solution.py:121
  109.8 9.6 collective-permute-start
  221.2 4.7 collective-permute-start.1
  327.7 6.2 collective-permute-start.2
  435.6 4.7 collective-permute-start.3
  542.1 124.0 %collective-permute-start.4 = (f32[64,64]{0,1:T(8,128)S(1)}, f32[64,64]{0,1:T(8,128)S(1)}, u32[]{:S(2)}, u32[]{:S(2)}) collective-permute-start(f32[64,64]{0,1:T(8,128)S(1)} %negate_bitcast_fusion.1), channel_id=1, source_target_pairs={{0,256},{256,0},{16,272},{272,16},{32,288},{288,32},{48,304},{304,... | collective-permute-start | bytes 49160 | tf_op jit(solution)/shard_map/ppermute | solution.py:16
  768.8 291.3 %copy-start.3 = (f32[384,64]{0,1:T(8,128)S(1)}, f32[384,64]{0,1:T(8,128)}, u32[]{:S(2)}) copy-start(f32[384,64]{0,1:T(8,128)} %param.23) | copy-start | bytes 294916
  768.8 291.9 %copy-start = (f32[384,768]{1,0:T(8,128)S(1)}, f32[384,768]{1,0:T(8,128)}, u32[]{:S(2)}) copy-start(f32[384,768]{1,0:T(8,128)} %param.22) | copy-start | bytes 3538948
  863.9 196.8 %copy-start.4 = (f32[64,64]{1,0:T(8,128)}, f32[64,64]{1,0:T(8,128)S(1)}, u32[]{:S(2)}) copy-start(f32[64,64]{1,0:T(8,128)S(1)} %get-tuple-element.1720) | copy-start | bytes 49156
  1060.7 1.6 copy-start.1
  1062.2 196.7 %all-gather.3.cloned.1.call-start = ((), (), s32[]{:S(2)}) async-start(), calls=%async_computation.1 | async-start | bytes 3244032 | tf_op jit(solution)/shard_map/all_gather | solution.py:114
  1063.0 318.6 %all-gather.5.cloned.1.call-start = ((), (), s32[]{:S(2)}) async-start(), calls=%async_computation.2 | async-start | bytes 3342336 | tf_op jit(solution)/shard_map/all_gather | solution.py:127
  1166.4 216.1 %copy-start.2 = (f32[384,64]{0,1:T(8,128)S(1)}, f32[384,64]{0,1:T(8,128)}, u32[]{:S(2)}) copy-start(f32[384,64]{0,1:T(8,128)} %copy-done.1) | copy-start | bytes 294916
Sparse Core Ops, SparseCore 0:
  1062.4 132.3 all-reduce.1
  1198.5 60.3 all-gather.2
  1305.0 76.5 all-gather.4
where the time goes:
time: 1410 us; the launch traced here: 1390 us
  matrix products  464 us (33%)
  loops' own time  277 us (20%)
  other arithmetic  262 us (19%)
  waiting for transfers between devices  179 us (13%)
  blocking collectives  165 us (12%)
  starting transfers between devices  16.6 us (1%)
  between operations  14.2 us (1%)
    dot_general x384, matrix products, one_column(): reduced = gram_column - jnp.dot(lower_part, earlier, precision=precise)  299 us
    another operation x6, loops' own time, upper_cholesky(): lax.fori_loop(0, order_now, one_column, jnp.zeros((order_now, order_now),...  274 us
    dot_general x192, matrix products, one_row(): jnp.dot(beyond, inverse_part, precision=precise)  154 us
    reduce_sum x192, other arithmetic, one_row(): diagonal_value = jnp.sum(jnp.where(positions == row_at, upper_row, 0.0))  123 us
    psum x1, blocking collectives, from_root(): return lax.psum(kept, axis)  122 us
    all_gather x1, waiting for transfers between devices, body(): lax.all_gather(corrected_cols, 'col', axis=0, tiled=True)  76.7 us
    all_gather x1, waiting for transfers between devices, body(): gathered_reflect = lax.all_gather(reflect_rows, 'row', axis=0, tiled=True)  62.8 us
    psum x1, blocking collectives, body(): inner_total = lax.psum(inner_part, 'col')  43.4 us
  transfers between devices with their start and end apart: 8, of which 7 were waited for; matrix products, arithmetic and copies ran while one was open for 8% of the time, Pallas kernels for 0%

commit v1 on v0

v1 whole, which is shorter than its diff:
```python
import jax
import jax.numpy as jnp
from jax import lax
from jax.experimental import pallas as pl
from jax.experimental.pallas import tpu as pltpu
from jax.sharding import PartitionSpec as P

F32 = jnp.float32
precise = lax.Precision.HIGHEST
ROWS, COLS, WIDTH = 384, 768, 64
PIECE = 24


def mm(a, b, ca=1, cb=0):
    return lax.dot_general(
        a, b, (((ca,), (cb,)), ((), ())), precision=precise, preferred_element_type=F32
    )


def spot(i):
    return (i % 4) * 4 + i // 4


def loop(lo, hi, step):
    lax.fori_loop(lo, hi, lambda i, carry: (step(i), carry)[1], 0)


def fold(block):
    return jnp.concatenate([block[:32], block[32:]], axis=1)


def unfold(block):
    return jnp.concatenate([block[:, :64], block[:, 64:]], axis=0)


def gather_kernel(
    a_hbm, p_hbm, band_ref, left_ref, dzb_ref, dp_ref,
    a_ref, p_ref, pe_ref, t_ref, t1_ref, tr_ref, zb_ref, zbr_ref, pp_ref,
    dzb, dp,
    gh_ref, gh1_ref, gr_ref, gx_ref, hx_ref, gs_ref,
    j_ref, j1_ref, jr_ref, jx_ref,
    gk, hh, ln, rk, lno,
    load_sem, one_send, one_recv,
    gs_sem, gr_sem, hs_sem, ts_sem, tr_sem, ps_sem, pr_sem, ds_sem, dr_sem,
    js_sem, jr_sem, us_sem, ur_sem, vs_sem, vr_sem,
):
    row = lax.axis_index("row")
    col = lax.axis_index("col")
    chip = row // 2
    core = row % 2
    other = 1 - core
    near = (chip * 2 + other, col)
    swap = (col * 2 + core, chip)

    load_p = pltpu.make_async_copy(p_hbm, p_ref, load_sem.at[0])
    load_a = pltpu.make_async_copy(a_hbm, a_ref, load_sem.at[1])
    load_p.start()
    load_a.start()

    def peer(d):
        return (chip + d) % 16

    def plane(i):
        return (i * 2 + core, col)

    def remote(src, dst, send, recv, device):
        return pltpu.make_async_remote_copy(
            src_ref=src, dst_ref=dst, send_sem=send, recv_sem=recv,
            device_id=device, device_id_type=pl.DeviceIdType.MESH,
        )

    def far(d):
        return (col % 4) + 4 * ((col // 4 + d) % 4)

    def close(d):
        return 4 * (col // 4) + (col % 4 + d) % 4

    barrier = pltpu.get_barrier_semaphore()

    def greet(device):
        pl.semaphore_signal(
            barrier, inc=1, device_id=device, device_id_type=pl.DeviceIdType.MESH
        )

    greet(near)
    loop(1, 16, lambda d: greet(plane(peer(d))))
    loop(1, 4, lambda d: greet((row, far(d))))
    loop(1, 4, lambda d: greet((row, close(d))))

    @pl.when(chip != col)
    def _():
        greet(swap)

    load_p.wait()
    panel = p_ref[...]
    rows_at = lax.broadcasted_iota(jnp.int32, (ROWS, WIDTH), 0)
    lanes_at = lax.broadcasted_iota(jnp.int32, (ROWS, WIDTH), 1)
    is_first = (row == 0).astype(F32)
    unit = jnp.where(rows_at == lanes_at, is_first, 0.0)
    pe_ref[...] = jnp.concatenate([panel, unit], axis=1)
    gram = mm(panel, panel, 0, 0)
    gh_ref[0] = fold(gram)
    gh_ref[1] = fold(panel[:WIDTH]) * is_first

    @pl.when(chip != col)
    def _():
        pl.semaphore_wait(barrier, 23)

    @pl.when(chip == col)
    def _():
        pl.semaphore_wait(barrier, 22)

    send_gh = remote(gh_ref, gh1_ref, one_send.at[0], one_recv.at[0], near)
    send_gh.start()

    send_pp = remote(
        p_ref.at[pl.ds(pl.multiple_of(PIECE * spot(col), 8), PIECE)],
        pp_ref, one_send.at[1], one_recv.at[1], swap,
    )
    keep_pp = pltpu.make_async_copy(
        p_ref.at[pl.ds(pl.multiple_of(PIECE * spot(col), 8), PIECE)], pp_ref, load_sem.at[2]
    )

    @pl.when(chip != col)
    def _():
        send_pp.start()

    @pl.when(chip == col)
    def _():
        keep_pp.start()

    load_a.wait()
    pe = pe_ref[...]
    for b in range(3):
        t_ref[256 * b : 256 * b + 256] = mm(a_ref[:, 256 * b : 256 * b + 256], pe, 0, 0)

    send_t = remote(
        t_ref.at[pl.ds(pl.multiple_of(other * ROWS, 8), ROWS)],
        t1_ref, one_send.at[2], one_recv.at[2], near,
    )
    send_t.start()

    send_gh.wait_recv()
    half = pl.ds(pl.multiple_of(core * 16, 8), 16)
    gs_ref[0] = gh_ref[0, half] + gh1_ref[0, half]
    gs_ref[1] = gh_ref[1, half] + gh1_ref[1, half]
    gr_ref[chip] = gs_ref[0]

    def send_gram(d):
        i = peer(d)
        remote(gs_ref.at[0], gr_ref.at[chip], gs_sem.at[i], gr_sem.at[chip], plane(i)).start()

    def send_head(d):
        i = peer(d)
        remote(gs_ref.at[1], hx_ref, hs_sem.at[i], one_recv.at[3], plane(i)).start()

    loop(1, 16, send_gram)

    @pl.when(chip == 0)
    def _():
        loop(1, 16, send_head)

    send_t.wait_recv()
    mine = pl.multiple_of(core * ROWS, 8)
    t_ref[pl.ds(mine, ROWS)] = t_ref[pl.ds(mine, ROWS)] + t1_ref[...]

    def t_piece(i):
        return t_ref.at[pl.ds(pl.multiple_of(core * ROWS + PIECE * spot(i), 8), PIECE)]

    def send_piece(d):
        i = peer(d)
        remote(t_piece(i), tr_ref.at[chip], ts_sem.at[i], tr_sem.at[chip], plane(i)).start()

    loop(1, 16, send_piece)
    tr_ref[chip] = t_ref[pl.ds(pl.multiple_of(core * ROWS + PIECE * spot(chip), 8), PIECE)]

    @pl.when(chip != col)
    def _():
        send_pp.wait_recv()

    @pl.when(chip == col)
    def _():
        keep_pp.wait()

    def place(i):
        return pl.ds(pl.multiple_of(core * ROWS + PIECE * spot(i), 8), PIECE)

    def send_rows(d):
        i = peer(d)
        remote(pp_ref, dp.at[place(chip)], ps_sem.at[i], pr_sem.at[chip], plane(i)).start()

    loop(1, 16, send_rows)
    dp[place(chip)] = pp_ref[...]

    def wait_gram(d):
        i = peer(d)
        remote(gs_ref.at[0], gr_ref.at[i], gs_sem.at[i], gr_sem.at[i], plane(i)).wait_recv()

    loop(1, 16, wait_gram)
    total = gr_ref[0]
    for i in range(1, 16):
        total = total + gr_ref[i]

    @pl.when(chip != 0)
    def _():
        remote(gs_ref.at[1], hx_ref, hs_sem.at[0], one_recv.at[3], plane(0)).wait_recv()

    @pl.when(chip == 0)
    def _():
        hx_ref[...] = gs_ref[1]

    gx_ref[0, half] = total
    gx_ref[1, half] = hx_ref[...]
    send_gx = remote(
        gx_ref.at[:, half], gx_ref.at[:, half], one_send.at[4], one_recv.at[4], near
    )
    send_gx.start()
    send_gx.wait_recv()

    gram = unfold(gx_ref[0])
    head = unfold(gx_ref[1])
    eye = jnp.where(
        lax.broadcasted_iota(jnp.int32, (64, 64), 0)
        == lax.broadcasted_iota(jnp.int32, (64, 64), 1), 1.0, 0.0,
    )
    gk[...] = jnp.concatenate([gram, eye], axis=1)
    hh[...] = jnp.concatenate([head, head.T], axis=1)
    ln[...] = jnp.concatenate([eye, eye], axis=1)

    lane = lax.broadcasted_iota(jnp.int32, (64, 128), 1)
    deep = lax.broadcasted_iota(jnp.int32, (64, 128), 0)
    lane1 = lax.broadcasted_iota(jnp.int32, (1, 128), 1)
    left = lane < 64
    left1 = lane1 < 64

    def column(j):
        at = pl.ds(j, 1)
        g_row, h_row, l_row = gk[at], hh[at], ln[at]
        g, h, l = gk[...], hh[...], ln[...]
        g_col = jnp.sum(jnp.where(lane == j, g, 0.0), axis=1, keepdims=True)
        h_col = jnp.sum(jnp.where(lane == j, h, 0.0), axis=1, keepdims=True)
        m_col = jnp.sum(jnp.where(lane == j + 64, h, 0.0), axis=1, keepdims=True)
        pivot = jnp.sum(jnp.where(lane1 == j, g_row, 0.0), axis=1, keepdims=True)
        entry = jnp.sum(jnp.where(lane1 == j, h_row, 0.0), axis=1, keepdims=True)
        inv = lax.rsqrt(pivot)
        inv = inv * (1.5 - 0.5 * pivot * inv * inv)
        scaled = g_row * inv
        turn = 1.0 / (entry + pivot * inv)
        rk[at] = -scaled
        gk[...] = g - (g_col * inv) * scaled
        factor = jnp.where(left, h_col * turn, m_col + g_col * inv)
        factor = jnp.where(deep > j, factor, 0.0)
        h_line = jnp.where(left1, h_row + scaled, h_row * turn)
        l_line = jnp.where(left1, l_row, l_row * turn)
        lno[at] = l_line
        hh[...] = h - factor * h_line
        ln[...] = l - factor * l_line

    loop(0, 16, column)

    def wait_piece(d):
        i = peer(d)
        remote(t_piece(i), tr_ref.at[i], ts_sem.at[i], tr_sem.at[i], plane(i)).wait_recv()

    loop(1, 16, wait_piece)
    total = tr_ref[0]
    for i in range(1, 16):
        total = total + tr_ref[i]
    zb_ref[...] = total

    def send_product(d):
        i = peer(d)
        remote(zb_ref, dzb.at[place(chip)], ds_sem.at[i], dr_sem.at[chip], plane(i)).start()

    there = pl.ds(pl.multiple_of(PIECE * spot(chip), 8), PIECE)
    here = pl.ds(pl.multiple_of(PIECE * spot(col), 8), PIECE)
    send_zb = remote(zb_ref, zbr_ref.at[there], one_send.at[5], one_recv.at[5], swap)

    @pl.when(chip != col)
    def _():
        send_zb.start()

    @pl.when(chip == col)
    def _():
        zbr_ref[there] = zb_ref[...]

    loop(1, 16, send_product)
    dzb[place(chip)] = zb_ref[...]

    loop(16, 32, column)

    @pl.when(chip != col)
    def _():
        send_zb.wait_recv()

    def send_far(d):
        i = (col // 4 + d) % 4
        remote(
            zbr_ref.at[here], zbr_ref.at[here], us_sem.at[i], ur_sem.at[col // 4], (row, far(d))
        ).start()

    loop(1, 4, send_far)

    loop(32, 48, column)

    def far_spot(i):
        return zbr_ref.at[pl.ds(pl.multiple_of(PIECE * ((col % 4) * 4 + i), 8), PIECE)]

    def wait_far(d):
        i = (col // 4 + d) % 4
        remote(far_spot(i), far_spot(i), us_sem.at[i], ur_sem.at[i], (row, far(d))).wait_recv()

    loop(1, 4, wait_far)

    def quarter(i):
        return zbr_ref.at[pl.ds(pl.multiple_of(4 * PIECE * i, 8), 4 * PIECE)]

    def send_close(d):
        i = (col % 4 + d) % 4
        remote(
            quarter(col % 4), quarter(col % 4), vs_sem.at[i], vr_sem.at[col % 4], (row, close(d))
        ).start()

    loop(1, 4, send_close)

    def wait_rows(d):
        i = peer(d)
        remote(pp_ref, dp.at[place(i)], ps_sem.at[i], pr_sem.at[i], plane(i)).wait_recv()
        remote(zb_ref, dzb.at[place(i)], ds_sem.at[i], dr_sem.at[i], plane(i)).wait_recv()

    loop(1, 16, wait_rows)
    own = pl.ds(mine, ROWS)
    send_dzb = remote(dzb.at[own], dzb.at[own], one_send.at[6], one_recv.at[6], near)
    send_dp = remote(dp.at[own], dp.at[own], one_send.at[7], one_recv.at[7], near)
    send_dzb.start()
    send_dp.start()

    loop(48, 64, column)

    band = jnp.where(
        lax.broadcasted_iota(jnp.int32, (64, 64), 0)
        <= lax.broadcasted_iota(jnp.int32, (64, 64), 1), rk[:, :64], 0.0,
    )
    band_ref[...] = band
    rs = -mm(lno[:, :64], lno[:, 64:], 0, 0)
    s = mm(rk[:, 64:], rs, 0, 0)

    def wait_close(d):
        i = (col % 4 + d) % 4
        remote(quarter(i), quarter(i), vs_sem.at[i], vr_sem.at[i], (row, close(d))).wait_recv()

    loop(1, 4, wait_close)
    first_rows = panel[:WIDTH] - is_first * band
    y = jnp.concatenate([first_rows, panel[WIDTH:]], axis=0)
    begun = mm(zbr_ref[...], jnp.concatenate([s, -rs], axis=0))
    inner = mm(mm(y, s), begun, 0, 0)

    j_ref[...] = fold(inner)
    send_j = remote(j_ref, j1_ref, one_send.at[8], one_recv.at[8], near)
    send_j.start()
    left_ref[:, :128] = jnp.concatenate([mm(y, s, 1, 1), -mm(y, rs, 1, 1)], axis=1)
    send_j.wait_recv()
    jr_ref[chip] = j_ref[half] + j1_ref[half]

    def send_inner(d):
        i = peer(d)
        remote(jr_ref.at[chip], jr_ref.at[chip], js_sem.at[i], jr_sem.at[chip], plane(i)).start()

    def wait_inner(d):
        i = peer(d)
        remote(jr_ref.at[i], jr_ref.at[i], js_sem.at[i], jr_sem.at[i], plane(i)).wait_recv()

    loop(1, 16, send_inner)
    send_dzb.wait_recv()
    send_dp.wait_recv()
    send_dzb.wait_send()
    send_dp.wait_send()
    dzb_ref[...] = dzb[...]
    dp_ref[...] = dp[...]
    loop(1, 16, wait_inner)
    total = jr_ref[0]
    for i in range(1, 16):
        total = total + jr_ref[i]
    jx_ref[half] = total
    send_jx = remote(jx_ref.at[half], jx_ref.at[half], one_send.at[9], one_recv.at[9], near)
    send_jx.start()
    send_jx.wait_recv()
    coupling = unfold(jx_ref[...])
    left_ref[:, 128:] = begun - mm(y, coupling)

    send_gh.wait_send()
    send_t.wait_send()
    send_gx.wait_send()
    send_j.wait_send()
    send_jx.wait_send()

    @pl.when(chip != col)
    def _():
        send_pp.wait_send()
        send_zb.wait_send()

    def sent(d):
        i = peer(d)
        remote(gs_ref.at[0], gr_ref.at[chip], gs_sem.at[i], gr_sem.at[chip], plane(i)).wait_send()
        remote(t_piece(i), tr_ref.at[chip], ts_sem.at[i], tr_sem.at[chip], plane(i)).wait_send()
        remote(pp_ref, dp.at[place(chip)], ps_sem.at[i], pr_sem.at[chip], plane(i)).wait_send()
        remote(zb_ref, dzb.at[place(chip)], ds_sem.at[i], dr_sem.at[chip], plane(i)).wait_send()
        remote(jr_ref.at[chip], jr_ref.at[chip], js_sem.at[i], jr_sem.at[chip], plane(i)).wait_send()

    loop(1, 16, sent)

    @pl.when(chip == 0)
    def _():
        def head_sent(d):
            i = peer(d)
            remote(gs_ref.at[1], hx_ref, hs_sem.at[i], one_recv.at[3], plane(i)).wait_send()

        loop(1, 16, head_sent)

    def z_sent(d):
        i = (col // 4 + d) % 4
        remote(
            zbr_ref.at[here], zbr_ref.at[here], us_sem.at[i], ur_sem.at[i], (row, far(d))
        ).wait_send()
        j = (col % 4 + d) % 4
        remote(
            quarter(col % 4), quarter(col % 4), vs_sem.at[j], vr_sem.at[j], (row, close(d))
        ).wait_send()

    loop(1, 4, z_sent)


def gathered(matrix, panel):
    dma = pltpu.SemaphoreType.DMA
    vmem = pltpu.VMEM
    return pl.pallas_call(
        gather_kernel,
        out_shape=(
            jax.ShapeDtypeStruct((WIDTH, WIDTH), F32),
            jax.ShapeDtypeStruct((ROWS, 192), F32),
            jax.ShapeDtypeStruct((COLS, 128), F32),
            jax.ShapeDtypeStruct((COLS, WIDTH), F32),
        ),
        in_specs=[pl.BlockSpec(memory_space=pl.ANY)] * 2,
        out_specs=[pl.BlockSpec(memory_space=pltpu.VMEM)] * 4,
        scratch_shapes=[
            vmem((ROWS, COLS), F32),
            vmem((ROWS, WIDTH), F32),
            vmem((ROWS, 128), F32),
            vmem((COLS, 128), F32),
            vmem((ROWS, 128), F32),
            vmem((16, PIECE, 128), F32),
            vmem((PIECE, 128), F32),
            vmem((ROWS, 128), F32),
            vmem((PIECE, WIDTH), F32),
            vmem((COLS, 128), F32),
            vmem((COLS, WIDTH), F32),
            vmem((2, 32, 128), F32),
            vmem((2, 32, 128), F32),
            vmem((16, 16, 128), F32),
            vmem((2, 32, 128), F32),
            vmem((16, 128), F32),
            vmem((2, 16, 128), F32),
            vmem((32, 128), F32),
            vmem((32, 128), F32),
            vmem((16, 16, 128), F32),
            vmem((32, 128), F32),
        ]
        + [vmem((64, 128), F32)] * 5
        + [dma((3,)), dma((10,)), dma((10,))]
        + [dma((16,))] * 11
        + [dma((4,))] * 4,
        compiler_params=pltpu.CompilerParams(
            collective_id=0, has_side_effects=True, vmem_limit_bytes=40 * 1024 * 1024
        ),
        cost_estimate=pl.CostEstimate(flops=10**9, bytes_accessed=10**7, transcendentals=0),
    )(matrix, panel)


def update_kernel(a_ref, left_ref, dzb_ref, dp_ref, band_ref, out_ref, band_out):
    first = (lax.axis_index("col") == 0).astype(F32)
    band = band_ref[...]
    band_out[...] = band
    top = dp_ref[:WIDTH] - first * band
    rows = jnp.concatenate([top, dp_ref[WIDTH:]], axis=0)
    right = jnp.concatenate([dzb_ref[...], rows], axis=1)
    left = left_ref[...]
    for b in range(3):
        part = slice(256 * b, 256 * b + 256)
        out_ref[:, part] = a_ref[:, part] - mm(left, right[part], 1, 1)


def body(matrix, panel):
    band, left, dzb, dp = gathered(matrix, panel)
    return pl.pallas_call(
        update_kernel,
        out_shape=(
            jax.ShapeDtypeStruct((ROWS, COLS), F32),
            jax.ShapeDtypeStruct((WIDTH, WIDTH), F32),
        ),
        compiler_params=pltpu.CompilerParams(vmem_limit_bytes=40 * 1024 * 1024),
        cost_estimate=pl.CostEstimate(flops=10**8, bytes_accessed=10**7, transcendentals=0),
    )(matrix, left, dzb, dp, band)


def solution(mesh):
    return jax.shard_map(
        body,
        mesh=mesh,
        in_specs=(P("row", "col"), P("row", None)),
        out_specs=(P("row", "col"), P()),
        check_vma=False,
    )
```

time: 1410 us -> 63.3 us (0.04); the launches traced: 1390 us -> 63.2 us
  matrix products: 464 us -> 0 us
  loops' own time: 277 us -> 0 us
  other arithmetic: 262 us -> 0 us
  waiting for transfers between devices: 179 us -> 0 us
  blocking collectives: 165 us -> 0 us
  Pallas kernels: 0 us -> 60.2 us
  starting transfers between devices: 16.6 us -> 0 us
    dot_general x597 -> x0, matrix products: 464 us -> none  [the longest x384 299 us: one_column(): reduced = gram_column - jnp.dot(lower_part, earlier, precision=precise)]
    another operation x10 -> x0, loops' own time: 277 us -> none  [the longest x6 274 us: upper_cholesky(): lax.fori_loop(0, order_now, one_column, jnp.zeros((order_now, order_now),...]
    psum x2 -> x0, blocking collectives: 165 us -> none  [the longest x1 122 us: from_root(): return lax.psum(kept, axis)]
    reduce_sum x256 -> x0, other arithmetic: 162 us -> none  [the longest x192 123 us: one_row(): diagonal_value = jnp.sum(jnp.where(positions == row_at, upper_row, 0.0))]
    all_gather x2 -> x0, waiting for transfers between devices: 140 us -> none  [the longest x1 76.7 us: body(): lax.all_gather(corrected_cols, 'col', axis=0, tiled=True)]
    pallas_call x0 -> x2, Pallas kernels: none -> 60.2 us  [the longest x1 58.1 us: gathered(): pl.pallas_call(gather_kernel, out_shape=(jax.ShapeDtypeStruct((WIDTH, WID...]
    select_n x578 -> x0, other arithmetic: 43.5 us -> none  [the longest x384 28.8 us: one_column(): jnp.where(positions[None, :] == column_index, new_column[:, None], lower_...]
    mul x64 -> x0, other arithmetic: 41.9 us -> none  [one_pivot(): working = working - multipliers[:, None] * pivot_row[None, :]]
  transfers between devices with their start and end apart: 8 -> 0, of which waited for: 7 -> 0; matrix products, arithmetic and copies ran while one was open for 8% -> 0% of each run, Pallas kernels for 0% -> 0%
where the time goes in v1:
time: 63.3 us; the launch traced here: 63.2 us
  Pallas kernels  60.2 us (95%)
  local copies, waits for them, and re-layouts  2.29 us (4%)
  between operations  0.65 us (1%)
    pallas_call x1, Pallas kernels, gathered(): pl.pallas_call(gather_kernel, out_shape=(jax.ShapeDtypeStruct((WIDTH, WID...  58.1 us
    unnamed x3, local copies, waits for them, and re-layouts  2.29 us
    pallas_call x1, Pallas kernels, body(): pl.pallas_call(update_kernel, out_shape=(jax.ShapeDtypeStruct((ROWS, COLS...  2.16 us

profile of v1, /device:TPU:1, one launch (start us, length us, event | category | flops | bytes accessed | tf_op | source)
XLA Modules:
  0.0 63.2 jit_solution(9724613968535920875)
XLA Ops:
  0.6 1.0 %copy.4.p_hbm = f32[384,64]{1,0:T(8,128)S(1)} copy(f32[384,64]{0,1:T(8,128)} %param.3) | data formatting | bytes 196608 | tf_op args[1]
  1.7 0.0 copy-start
  1.7 1.3 %copy-done = f32[384,768]{1,0:T(8,128)S(1)} copy-done((f32[384,768]{1,0:T(8,128)S(1)}, f32[384,768]{1,0:T(8,128)}, u32[]{:S(2)}) %copy-start) | copy-done | bytes 1179672
  2.9 58.1 %shard_map.41 = (f32[64,64]{1,0:T(8,128)S(1)}, f32[384,192]{1,0:T(8,128)S(1)}, f32[768,128]{1,0:T(8,128)S(1)}, f32[768,64]{1,0:T(8,128)S(1)}) custom-call(f32[384,768]{1,0:T(8,128)S(1)} %copy-done, f32[384,64]{1,0:T(8,128)S(1)} %copy.4.p_hbm), custom_call_target="tpu_custom_call" | custom-call | flops 1000000000 | bytes 10000000 | tf_op jit(solution)/shard_map/pallas_call | solution.py:436
  61.0 2.2 %shard_map.42 = (f32[384,768]{1,0:T(8,128)}, f32[64,64]{1,0:T(8,128)}) custom-call(f32[384,768]{1,0:T(8,128)S(1)} %copy-done, f32[384,192]{1,0:T(8,128)S(1)} %get-tuple-element.6.left_ref, f32[768,128]{1,0:T(8,128)S(1)} %get-tuple-element.7.dzb_ref, f32[768,64]{1,0:T(8,128)S(1)} %get-tuple-element.8.dp_ref, f32[64,64]{1,0:T(8,128)S(1)} %get-tuple-element.9.band_ref), custom_call_target="tpu_custom_call" | custom-call | flops 100000000 | bytes 10000000 | tf_op jit(solution)/shard_map/pallas_call | solution.py:495
Async XLA Ops:
  1.7 1.3 %copy-start = (f32[384,768]{1,0:T(8,128)S(1)}, f32[384,768]{1,0:T(8,128)}, u32[]{:S(2)}) copy-start(f32[384,768]{1,0:T(8,128)} %a_ref.1) | copy-start | bytes 3538948

commit v2 on v1

v2 whole, which is shorter than its diff:
```python
import jax
import jax.numpy as jnp
from jax import lax
from jax.experimental import pallas as pl
from jax.experimental.pallas import tpu as pltpu
from jax.sharding import PartitionSpec as P

F32 = jnp.float32
precise = lax.Precision.HIGHEST
ROWS, COLS, WIDTH = 384, 768, 64
SLAB = 12
HALF = 192


def mm(a, b, ca=1, cb=0):
    return lax.dot_general(
        a, b, (((ca,), (cb,)), ((), ())), precision=precise, preferred_element_type=F32
    )


def loop(lo, hi, step):
    lax.fori_loop(lo, hi, lambda i, carry: (step(i), carry)[1], 0)


def fold(block):
    rows = block.shape[0] // 2
    return jnp.concatenate([block[:rows], block[rows:]], axis=1)


def unfold(block):
    return jnp.concatenate([block[:, :64], block[:, 64:]], axis=0)


def to_slabs(ref, lead, block):
    folded = fold(block)
    for i in range(16):
        ref[lead + i] = folded[SLAB * i : SLAB * i + SLAB]


def from_slabs(ref, lead):
    return unfold(jnp.concatenate([ref[lead + i] for i in range(16)], axis=0))


def gather_kernel(
    a_hbm, p_hbm, band_ref, base_ref, yj_ref, yc_ref,
    a_ref, pt_ref, p3, pp_ref, t3, t1, tr, zs, b3, bs, d3, zr, br,
    gh_ref, gh1_ref, gr_ref, gx_ref, hx_ref, gs_ref,
    j_ref, j1_ref, jr_ref, jx_ref,
    gk, hh, ln, rk, lno,
    load_sem, one_send, one_recv,
    gs_sem, gr_sem, hs_sem, ts_sem, tr_sem, bs_sem,
    zs_sem, zr_sem, ys_sem, yr_sem, js_sem, jr_sem, ds_sem, dr_sem,
):
    row = lax.axis_index("row")
    col = lax.axis_index("col")
    chip = row // 2
    core = row % 2
    other = 1 - core
    near = (chip * 2 + other, col)
    swap = (col * 2 + core, chip)

    loads = [pltpu.make_async_copy(p_hbm, pt_ref, load_sem.at[0])]
    for b in range(3):
        cut = pl.ds(256 * b, 256)
        loads.append(pltpu.make_async_copy(a_hbm.at[:, cut], a_ref.at[:, cut], load_sem.at[1 + b]))
    for load in loads:
        load.start()

    def peer(d):
        return (chip + d) % 16

    def plane(i):
        return (i * 2 + core, col)

    def remote(src, dst, send, recv, device):
        return pltpu.make_async_remote_copy(
            src_ref=src, dst_ref=dst, send_sem=send, recv_sem=recv,
            device_id=device, device_id_type=pl.DeviceIdType.MESH,
        )

    barrier = pltpu.get_barrier_semaphore()

    def greet(device):
        pl.semaphore_signal(
            barrier, inc=1, device_id=device, device_id_type=pl.DeviceIdType.MESH
        )

    loop(1, 16, lambda d: greet((peer(d) * 2 + core, chip)))

    @pl.when(chip != col)
    def _():
        greet((row, chip))

    loop(1, 16, lambda d: greet(plane(peer(d))))
    greet(near)

    loads[0].wait()
    pt = pt_ref[...]
    panel = pt.T
    is_first = (row == 0).astype(F32)
    gh_ref[0] = fold(mm(pt, pt, 1, 1))
    gh_ref[1] = fold(panel[:WIDTH]) * is_first
    to_slabs(p3, 0, panel)
    parts = []
    for b in range(3):
        loads[1 + b].wait()
        parts.append(mm(pt, a_ref[:, 256 * b : 256 * b + 256]).T)
    partial = jnp.concatenate(parts, axis=0)
    to_slabs(t3, 0, partial[:ROWS])
    to_slabs(t3, 16, partial[ROWS:])

    @pl.when(row == 0)
    def _():
        first_columns = a_ref[:WIDTH].T
        to_slabs(b3, 0, first_columns[:ROWS])
        to_slabs(b3, 16, first_columns[ROWS:])

    @pl.when(chip != col)
    def _():
        pl.semaphore_wait(barrier, 32)

    @pl.when(chip == col)
    def _():
        pl.semaphore_wait(barrier, 31)

    send_gh = remote(gh_ref, gh1_ref, one_send.at[0], one_recv.at[0], near)
    send_gh.start()
    send_t = remote(t3.at[pl.ds(other * 16, 16)], t1, one_send.at[2], one_recv.at[2], near)
    send_t.start()

    send_pp = remote(p3.at[col], pp_ref, one_send.at[1], one_recv.at[1], swap)

    @pl.when(chip != col)
    def _():
        send_pp.start()

    send_b = remote(
        b3.at[pl.ds(16, 16)], b3.at[pl.ds(16, 16)], one_send.at[3], one_recv.at[3], near
    )

    @pl.when(row == 0)
    def _():
        send_b.start()

    send_gh.wait_recv()
    half = pl.ds(pl.multiple_of(core * 16, 8), 16)
    gs_ref[0] = gh_ref[0, half] + gh1_ref[0, half]
    gs_ref[1] = gh_ref[1, half] + gh1_ref[1, half]

    def send_gram(d):
        i = peer(d)
        remote(gs_ref.at[0], gr_ref.at[chip], gs_sem.at[i], gr_sem.at[chip], plane(i)).start()

    def send_head(d):
        i = peer(d)
        remote(gs_ref.at[1], hx_ref, hs_sem.at[i], one_recv.at[5], plane(i)).start()

    loop(1, 16, send_gram)

    @pl.when(chip == 0)
    def _():
        loop(1, 16, send_head)

    gr_ref[chip] = gs_ref[0]

    send_t.wait_recv()
    mine = pl.ds(core * 16, 16)
    t3[mine] = t3[mine] + t1[...]

    def send_part(d):
        i = peer(d)
        remote(t3.at[core * 16 + i], tr.at[chip], ts_sem.at[i], tr_sem.at[chip], plane(i)).start()

    loop(1, 16, send_part)
    tr[chip] = t3[core * 16 + chip]

    @pl.when(row == 1)
    def _():
        send_b.wait_recv()

    def send_first(d):
        i = peer(d)
        remote(b3.at[core * 16 + i], bs, bs_sem.at[i], one_recv.at[6], plane(i)).start()

    @pl.when(chip == 0)
    def _():
        loop(1, 16, send_first)
        bs[...] = b3[core * 16]

    def wait_gram(d):
        i = peer(d)
        remote(gs_ref.at[0], gr_ref.at[i], gs_sem.at[i], gr_sem.at[i], plane(i)).wait_recv()

    loop(1, 16, wait_gram)
    total = gr_ref[0]
    for i in range(1, 16):
        total = total + gr_ref[i]

    @pl.when(chip != 0)
    def _():
        remote(gs_ref.at[1], hx_ref, hs_sem.at[0], one_recv.at[5], plane(0)).wait_recv()

    @pl.when(chip == 0)
    def _():
        hx_ref[...] = gs_ref[1]

    gx_ref[0, half] = total
    gx_ref[1, half] = hx_ref[...]
    send_gx = remote(
        gx_ref.at[:, half], gx_ref.at[:, half], one_send.at[4], one_recv.at[4], near
    )
    send_gx.start()

    slot = core * 16 + chip

    def spread(src, dst, send, recv):
        def step(d):
            z = (col + d) % 16
            remote(src, dst.at[chip], send.at[z], recv.at[chip], (col * 2 + core, z)).start()

        loop(1, 16, step)

        @pl.when(chip != col)
        def _():
            step(0)

        @pl.when(chip == col)
        def _():
            dst[chip] = src[...]

    def share(which, src):
        def step(d):
            i = peer(d)
            remote(
                src, d3.at[which, slot], ds_sem.at[which, i], dr_sem.at[which, chip], plane(i)
            ).start()

        loop(1, 16, step)
        d3[which, slot] = src[...]

    def wait_part(d):
        i = peer(d)
        remote(t3.at[core * 16 + i], tr.at[i], ts_sem.at[i], tr_sem.at[i], plane(i)).wait_recv()

    loop(1, 16, wait_part)
    total = tr[0]
    for i in range(1, 16):
        total = total + tr[i]
    zs[...] = total
    spread(zs, zr, zs_sem, zr_sem)

    @pl.when(chip != 0)
    def _():
        remote(b3.at[core * 16], bs, bs_sem.at[0], one_recv.at[6], plane(0)).wait_recv()

    spread(bs, br, ys_sem, yr_sem)
    share(0, zs)
    share(1, bs)

    send_gx.wait_recv()
    gram = unfold(gx_ref[0])
    head = unfold(gx_ref[1])
    eye = jnp.where(
        lax.broadcasted_iota(jnp.int32, (64, 64), 0)
        == lax.broadcasted_iota(jnp.int32, (64, 64), 1), 1.0, 0.0,
    )
    gk[...] = jnp.concatenate([gram, eye], axis=1)
    hh[...] = jnp.concatenate([head, head.T], axis=1)
    ln[...] = jnp.concatenate([eye, eye], axis=1)

    lane = lax.broadcasted_iota(jnp.int32, (64, 128), 1)
    deep = lax.broadcasted_iota(jnp.int32, (64, 128), 0)
    lane1 = lax.broadcasted_iota(jnp.int32, (1, 128), 1)
    left = lane < 64
    left1 = lane1 < 64

    def column(j):
        at = pl.ds(j, 1)
        g_row, h_row, l_row = gk[at], hh[at], ln[at]
        g, h, l = gk[...], hh[...], ln[...]
        g_col = jnp.sum(jnp.where(lane == j, g, 0.0), axis=1, keepdims=True)
        h_col = jnp.sum(jnp.where(lane == j, h, 0.0), axis=1, keepdims=True)
        m_col = jnp.sum(jnp.where(lane == j + 64, h, 0.0), axis=1, keepdims=True)
        pivot = jnp.sum(jnp.where(lane1 == j, g_row, 0.0), axis=1, keepdims=True)
        entry = jnp.sum(jnp.where(lane1 == j, h_row, 0.0), axis=1, keepdims=True)
        inv = lax.rsqrt(pivot)
        inv = inv * (1.5 - 0.5 * pivot * inv * inv)
        scaled = g_row * inv
        turn = 1.0 / (entry + pivot * inv)
        rk[at] = -scaled
        gk[...] = g - (g_col * inv) * scaled
        factor = jnp.where(left, h_col * turn, m_col + g_col * inv)
        factor = jnp.where(deep > j, factor, 0.0)
        h_line = jnp.where(left1, h_row + scaled, h_row * turn)
        l_line = jnp.where(left1, l_row, l_row * turn)
        lno[at] = l_line
        hh[...] = h - factor * h_line
        ln[...] = l - factor * l_line

    loop(0, 24, column)

    @pl.when(chip != col)
    def _():
        send_pp.wait_recv()

    @pl.when(chip == col)
    def _():
        pp_ref[...] = p3[col]

    share(2, pp_ref)
    loop(24, 64, column)

    band = jnp.where(
        lax.broadcasted_iota(jnp.int32, (64, 64), 0)
        <= lax.broadcasted_iota(jnp.int32, (64, 64), 1), rk[:, :64], 0.0,
    )
    band_ref[...] = band
    rs = -mm(lno[:, :64], lno[:, 64:], 0, 0)
    s = mm(rk[:, 64:], rs, 0, 0)

    def wait_rows(d):
        i = peer(d)
        for which in range(3):
            to = d3.at[which, core * 16 + i]
            remote(to, to, ds_sem.at[which, i], dr_sem.at[which, i], plane(i)).wait_recv()

    loop(1, 16, wait_rows)
    own = d3.at[:, mine]
    send_d = remote(own, own, one_send.at[6], one_recv.at[7], near)
    send_d.start()

    y = jnp.concatenate([panel[:WIDTH] - is_first * band, panel[WIDTH:]], axis=0)
    ys = mm(y, s)
    spread_left = jnp.concatenate([mm(y, s, 1, 1), -mm(y, rs, 1, 1)], axis=1)
    maps = jnp.concatenate([s, -rs], axis=0)

    def wait_spread(d):
        i = peer(d)
        remote(zs, zr.at[i], zs_sem.at[i], zr_sem.at[i], swap).wait_recv()
        remote(bs, br.at[i], ys_sem.at[i], yr_sem.at[i], swap).wait_recv()

    loop(1, 16, wait_spread)

    @pl.when(chip != col)
    def _():
        wait_spread(0)

    begun = mm(jnp.concatenate([from_slabs(zr, 0), from_slabs(br, 0)], axis=1), maps)
    inner = mm(ys, begun, 0, 0)

    j_ref[...] = fold(inner)
    send_j = remote(j_ref, j1_ref, one_send.at[8], one_recv.at[8], near)
    send_j.start()
    send_j.wait_recv()
    jr_ref[chip] = j_ref[half] + j1_ref[half]

    def send_inner(d):
        i = peer(d)
        remote(jr_ref.at[chip], jr_ref.at[chip], js_sem.at[i], jr_sem.at[chip], plane(i)).start()

    def wait_inner(d):
        i = peer(d)
        remote(jr_ref.at[i], jr_ref.at[i], js_sem.at[i], jr_sem.at[i], plane(i)).wait_recv()

    loop(1, 16, send_inner)

    send_d.wait_recv()
    send_d.wait_send()
    rights = []
    for which in range(3):
        rights.append(jnp.concatenate([from_slabs(d3.at[which], 0), from_slabs(d3.at[which], 16)], axis=0))
    zero_col = (col == 0).astype(F32)
    yc = jnp.concatenate([rights[2][:WIDTH] - zero_col * band, rights[2][WIDTH:]], axis=0)
    yc_ref[...] = yc
    right = jnp.concatenate([rights[0], rights[1], yc], axis=1)
    whole_left = jnp.concatenate([spread_left, begun], axis=1)
    for b in range(3):
        cut = slice(256 * b, 256 * b + 256)
        base_ref[:, cut] = a_ref[:, cut] - mm(whole_left, right[cut], 1, 1)

    loop(1, 16, wait_inner)
    total = jr_ref[0]
    for i in range(1, 16):
        total = total + jr_ref[i]
    jx_ref[half] = total
    send_jx = remote(jx_ref.at[half], jx_ref.at[half], one_send.at[9], one_recv.at[9], near)
    send_jx.start()

    send_gh.wait_send()
    send_t.wait_send()
    send_gx.wait_send()
    send_j.wait_send()

    @pl.when(chip != col)
    def _():
        send_pp.wait_send()

    @pl.when(row == 0)
    def _():
        send_b.wait_send()

    def sent(d):
        i = peer(d)
        remote(gs_ref.at[0], gr_ref.at[chip], gs_sem.at[i], gr_sem.at[chip], plane(i)).wait_send()
        remote(t3.at[i], tr.at[chip], ts_sem.at[i], tr_sem.at[chip], plane(i)).wait_send()
        remote(jr_ref.at[chip], jr_ref.at[chip], js_sem.at[i], jr_sem.at[chip], plane(i)).wait_send()
        for which in range(3):
            remote(zs, zs, ds_sem.at[which, i], dr_sem.at[which, i], plane(i)).wait_send()

    loop(1, 16, sent)

    @pl.when(chip == 0)
    def _():
        def head_sent(d):
            i = peer(d)
            remote(gs_ref.at[1], hx_ref, hs_sem.at[i], one_recv.at[5], plane(i)).wait_send()
            remote(b3.at[i], bs, bs_sem.at[i], one_recv.at[6], plane(i)).wait_send()

        loop(1, 16, head_sent)

    def spread_sent(d):
        z = (col + d) % 16
        remote(zs, zr.at[chip], zs_sem.at[z], zr_sem.at[chip], swap).wait_send()
        remote(bs, br.at[chip], ys_sem.at[z], yr_sem.at[chip], swap).wait_send()

    loop(1, 16, spread_sent)

    @pl.when(chip != col)
    def _():
        spread_sent(0)

    send_jx.wait_recv()
    yj_ref[...] = mm(y, unfold(jx_ref[...]))
    send_jx.wait_send()


def gathered(matrix, panel):
    dma = pltpu.SemaphoreType.DMA
    vmem = pltpu.VMEM
    slabs = lambda *lead: vmem((*lead, SLAB, 128), F32)
    return pl.pallas_call(
        gather_kernel,
        out_shape=(
            jax.ShapeDtypeStruct((WIDTH, WIDTH), F32),
            jax.ShapeDtypeStruct((ROWS, COLS), F32),
            jax.ShapeDtypeStruct((ROWS, WIDTH), F32),
            jax.ShapeDtypeStruct((COLS, WIDTH), F32),
        ),
        in_specs=[pl.BlockSpec(memory_space=pltpu.HBM)] * 2,
        out_specs=[pl.BlockSpec(memory_space=pltpu.VMEM)] * 4,
        scratch_shapes=[
            vmem((ROWS, COLS), F32),
            vmem((WIDTH, ROWS), F32),
            slabs(16), slabs(), slabs(32), slabs(16), slabs(16), slabs(),
            slabs(32), slabs(), slabs(3, 32), slabs(16), slabs(16),
            vmem((2, 32, 128), F32),
            vmem((2, 32, 128), F32),
            vmem((16, 16, 128), F32),
            vmem((2, 32, 128), F32),
            vmem((16, 128), F32),
            vmem((2, 16, 128), F32),
            vmem((32, 128), F32),
            vmem((32, 128), F32),
            vmem((16, 16, 128), F32),
            vmem((32, 128), F32),
        ]
        + [vmem((64, 128), F32)] * 5
        + [dma((4,)), dma((10,)), dma((10,))]
        + [dma((16,))] * 12
        + [dma((3, 16))] * 2,
        compiler_params=pltpu.CompilerParams(
            collective_id=0, has_side_effects=True, vmem_limit_bytes=40 * 1024 * 1024
        ),
        cost_estimate=pl.CostEstimate(flops=10**9, bytes_accessed=10**7, transcendentals=0),
    )(matrix, panel.T)


def update_kernel(base_ref, yj_ref, yc_ref, band_ref, out_ref, band_out):
    band_out[...] = band_ref[...]
    yj = yj_ref[...]
    for b in range(3):
        cut = slice(256 * b, 256 * b + 256)
        out_ref[:, cut] = base_ref[:, cut] + mm(yj, yc_ref[cut], 1, 1)


def body(matrix, panel):
    band, base, yj, yc = gathered(matrix, panel)
    return pl.pallas_call(
        update_kernel,
        out_shape=(
            jax.ShapeDtypeStruct((ROWS, COLS), F32),
            jax.ShapeDtypeStruct((WIDTH, WIDTH), F32),
        ),
        compiler_params=pltpu.CompilerParams(vmem_limit_bytes=40 * 1024 * 1024),
        cost_estimate=pl.CostEstimate(flops=10**8, bytes_accessed=10**7, transcendentals=0),
    )(base, yj, yc, band)


def solution(mesh):
    return jax.shard_map(
        body,
        mesh=mesh,
        in_specs=(P("row", "col"), P("row", None)),
        out_specs=(P("row", "col"), P()),
        check_vma=False,
    )
```

time: 63.3 us -> 55.5 us (0.88)
  Pallas kernels: 60.2 us -> 52.5 us
    pallas_call x1, Pallas kernels: 58.1 us -> 50.4 us  [gathered(): pl.pallas_call(gather_kernel, out_shape=(jax.ShapeDtypeStruct((WIDTH, WID...]
    unnamed x3 -> x4, local copies, waits for them, and re-layouts: 2.29 us -> 2.16 us
where the time goes in v2:
time: 55.5 us; the launch traced here: 55.3 us
  Pallas kernels  52.5 us (95%)
  local copies, waits for them, and re-layouts  2.16 us (4%)
  between operations  0.65 us (1%)
    pallas_call x1, Pallas kernels, gathered(): pl.pallas_call(gather_kernel, out_shape=(jax.ShapeDtypeStruct((WIDTH, WID...  50.4 us
    unnamed x4, local copies, waits for them, and re-layouts  2.16 us
    pallas_call x1, Pallas kernels, body(): pl.pallas_call(update_kernel, out_shape=(jax.ShapeDtypeStruct((ROWS, COLS...  2.11 us

profile of v2, /device:TPU:1, one launch (start us, length us, event | category | flops | bytes accessed | tf_op | source)
XLA Modules:
  0.0 55.3 jit_solution(18098323430632700934)
XLA Ops:
  0.6 0.0 copy-start
  0.6 1.3 %copy-done = f32[384,768]{1,0:T(8,128)S(1)} copy-done((f32[384,768]{1,0:T(8,128)S(1)}, f32[384,768]{1,0:T(8,128)}, u32[]{:S(2)}) %copy-start) | copy-done | bytes 1179672
  1.9 0.0 copy-start.1
  1.9 0.9 %copy-done.1 = f32[384,64]{0,1:T(8,128)S(1)} copy-done((f32[384,64]{0,1:T(8,128)S(1)}, f32[384,64]{0,1:T(8,128)}, u32[]{:S(2)}) %copy-start.1) | copy-done | bytes 98328
  2.8 50.4 %shard_map.41 = (f32[64,64]{1,0:T(8,128)S(1)}, f32[384,768]{1,0:T(8,128)S(1)}, f32[384,64]{1,0:T(8,128)S(1)}, f32[768,64]{1,0:T(8,128)S(1)}) custom-call(f32[384,768]{1,0:T(8,128)S(1)} %copy-done, f32[64,384]{1,0:T(8,128)S(1)} %bitcast.1), custom_call_target="tpu_custom_call" | custom-call | flops 1000000000 | bytes 10000000 | tf_op jit(solution)/shard_map/pallas_call | solution.py:441
  53.2 2.1 %shard_map.42 = (f32[384,768]{1,0:T(8,128)}, f32[64,64]{1,0:T(8,128)}) custom-call(f32[384,768]{1,0:T(8,128)S(1)} %get-tuple-element.6.base_ref, f32[384,64]{1,0:T(8,128)S(1)} %get-tuple-element.7.yj_ref, f32[768,64]{1,0:T(8,128)S(1)} %get-tuple-element.8.yc_ref, f32[64,64]{1,0:T(8,128)S(1)} %get-tuple-element.9.band_ref), custom_call_target="tpu_custom_call" | custom-call | flops 100000000 | bytes 10000000 | tf_op jit(solution)/shard_map/pallas_call | solution.py:488
Async XLA Ops:
  0.6 1.3 %copy-start = (f32[384,768]{1,0:T(8,128)S(1)}, f32[384,768]{1,0:T(8,128)}, u32[]{:S(2)}) copy-start(f32[384,768]{1,0:T(8,128)} %a_hbm.1) | copy-start | bytes 3538948
  1.9 0.9 %copy-start.1 = (f32[384,64]{0,1:T(8,128)S(1)}, f32[384,64]{0,1:T(8,128)}, u32[]{:S(2)}) copy-start(f32[384,64]{0,1:T(8,128)} %param.3) | copy-start | bytes 294916

commit v3 on v2

--- a/solution.py
+++ b/solution.py
@@ -18,6 +18,19 @@
     )
 
 
+def halves(x):
+    high = x.astype(jnp.bfloat16)
+    return high, (x - high.astype(F32)).astype(jnp.bfloat16)
+
+
+def mm3(a, b):
+    (ah, al), (bh, bl) = a, b
+    dot = lambda u, v: lax.dot_general(
+        u, v, (((1,), (1,)), ((), ())), preferred_element_type=F32
+    )
+    return dot(ah, bh) + (dot(ah, bl) + dot(al, bh))
+
+
 def loop(lo, hi, step):
     lax.fori_loop(lo, hi, lambda i, carry: (step(i), carry)[1], 0)
 
@@ -37,13 +50,13 @@
         ref[lead + i] = folded[SLAB * i : SLAB * i + SLAB]
 
 
-def from_slabs(ref, lead):
-    return unfold(jnp.concatenate([ref[lead + i] for i in range(16)], axis=0))
+def from_slabs(read):
+    return unfold(jnp.concatenate([read(i) for i in range(16)], axis=0))
 
 
 def gather_kernel(
     a_hbm, p_hbm, band_ref, base_ref, yj_ref, yc_ref,
-    a_ref, pt_ref, p3, pp_ref, t3, t1, tr, zs, b3, bs, d3, zr, br,
+    a_ref, pt_ref, p3, t3, t1, tr, own3, b3, d3, zr, br,
     gh_ref, gh1_ref, gr_ref, gx_ref, hx_ref, gs_ref,
     j_ref, j1_ref, jr_ref, jx_ref,
     gk, hh, ln, rk, lno,
@@ -59,6 +72,7 @@
     near = (chip * 2 + other, col)
     swap = (col * 2 + core, chip)
 
+    zs, bs, pp_ref = own3.at[0], own3.at[1], own3.at[2]
     loads = [pltpu.make_async_copy(p_hbm, pt_ref, load_sem.at[0])]
     for b in range(3):
         cut = pl.ds(256 * b, 256)
@@ -93,6 +107,12 @@
 
     loop(1, 16, lambda d: greet(plane(peer(d))))
     greet(near)
+
+    @pl.when(chip > 0)
+    def _():
+        @pl.when(core == 1)
+        def _():
+            greet((0, col))
 
     loads[0].wait()
     pt = pt_ref[...]
@@ -109,19 +129,25 @@
     to_slabs(t3, 0, partial[:ROWS])
     to_slabs(t3, 16, partial[ROWS:])
 
+    @pl.when(row > 0)
+    def _():
+        @pl.when(chip != col)
+        def _():
+            pl.semaphore_wait(barrier, 32)
+
+        @pl.when(chip == col)
+        def _():
+            pl.semaphore_wait(barrier, 31)
+
     @pl.when(row == 0)
     def _():
-        first_columns = a_ref[:WIDTH].T
-        to_slabs(b3, 0, first_columns[:ROWS])
-        to_slabs(b3, 16, first_columns[ROWS:])
-
-    @pl.when(chip != col)
-    def _():
-        pl.semaphore_wait(barrier, 32)
-
-    @pl.when(chip == col)
-    def _():
-        pl.semaphore_wait(barrier, 31)
+        @pl.when(col > 0)
+        def _():
+            pl.semaphore_wait(barrier, 47)
+
+        @pl.when(col == 0)
+        def _():
+            pl.semaphore_wait(barrier, 46)
 
     send_gh = remote(gh_ref, gh1_ref, one_send.at[0], one_recv.at[0], near)
     send_gh.start()
@@ -134,13 +160,19 @@
     def _():
         send_pp.start()
 
-    send_b = remote(
-        b3.at[pl.ds(16, 16)], b3.at[pl.ds(16, 16)], one_send.at[3], one_recv.at[3], near
-    )
+    def first_slab(i, k):
+        return remote(
+            b3.at[k * 16 + i], bs, bs_sem.at[k * 16 + i], one_recv.at[6], (i * 2 + k, col)
+        )
 
     @pl.when(row == 0)
     def _():
-        send_b.start()
+        first_columns = a_ref[:WIDTH].T
+        to_slabs(b3, 0, first_columns[:ROWS])
+        to_slabs(b3, 16, first_columns[ROWS:])
+        loop(1, 16, lambda i: first_slab(i, 0).start())
+        loop(0, 16, lambda i: first_slab(i, 1).start())
+        bs[...] = b3[0]
 
     send_gh.wait_recv()
     half = pl.ds(pl.multiple_of(core * 16, 8), 16)
@@ -174,18 +206,28 @@
     loop(1, 16, send_part)
     tr[chip] = t3[core * 16 + chip]
 
-    @pl.when(row == 1)
-    def _():
-        send_b.wait_recv()
-
-    def send_first(d):
-        i = peer(d)
-        remote(b3.at[core * 16 + i], bs, bs_sem.at[i], one_recv.at[6], plane(i)).start()
-
-    @pl.when(chip == 0)
-    def _():
-        loop(1, 16, send_first)
-        bs[...] = b3[core * 16]
+    slot = core * 16 + chip
+
+    def spread(src, dst, send, recv):
+        def step(d):
+            z = (col + d) % 16
+            remote(src, dst.at[chip], send.at[z], recv.at[chip], (col * 2 + core, z)).start()
+
+        loop(1, 16, step)
+
+        @pl.when(chip != col)
+        def _():
+            step(0)
+
+        @pl.when(chip == col)
+        def _():
+            dst[chip] = src[...]
+
+    @pl.when(row > 0)
+    def _():
+        first_slab(0, 0).wait_recv()
+
+    spread(bs, br, ys_sem, yr_sem)
 
     def wait_gram(d):
         i = peer(d)
@@ -211,33 +253,6 @@
     )
     send_gx.start()
 
-    slot = core * 16 + chip
-
-    def spread(src, dst, send, recv):
-        def step(d):
-            z = (col + d) % 16
-            remote(src, dst.at[chip], send.at[z], recv.at[chip], (col * 2 + core, z)).start()
-
-        loop(1, 16, step)
-
-        @pl.when(chip != col)
-        def _():
-            step(0)
-
-        @pl.when(chip == col)
-        def _():
-            dst[chip] = src[...]
-
-    def share(which, src):
-        def step(d):
-            i = peer(d)
-            remote(
-                src, d3.at[which, slot], ds_sem.at[which, i], dr_sem.at[which, chip], plane(i)
-            ).start()
-
-        loop(1, 16, step)
-        d3[which, slot] = src[...]
-
     def wait_part(d):
         i = peer(d)
         remote(t3.at[core * 16 + i], tr.at[i], ts_sem.at[i], tr_sem.at[i], plane(i)).wait_recv()
@@ -248,14 +263,6 @@
         total = total + tr[i]
     zs[...] = total
     spread(zs, zr, zs_sem, zr_sem)
-
-    @pl.when(chip != 0)
-    def _():
-        remote(b3.at[core * 16], bs, bs_sem.at[0], one_recv.at[6], plane(0)).wait_recv()
-
-    spread(bs, br, ys_sem, yr_sem)
-    share(0, zs)
-    share(1, bs)
 
     send_gx.wait_recv()
     gram = unfold(gx_ref[0])
@@ -274,30 +281,54 @@
     left = lane < 64
     left1 = lane1 < 64
 
-    def column(j):
-        at = pl.ds(j, 1)
-        g_row, h_row, l_row = gk[at], hh[at], ln[at]
+    def pick(x, at, j):
+        return jnp.sum(jnp.where(at == j, x, 0.0), axis=1, keepdims=True)
+
+    def inverse_root(x):
+        guess = lax.rsqrt(x)
+        return guess * (1.5 - 0.5 * x * guess * guess)
+
+    def pair(step):
+        j = 2 * step
+        i = j + 1
+        one, two = pl.ds(j, 1), pl.ds(i, 1)
         g, h, l = gk[...], hh[...], ln[...]
-        g_col = jnp.sum(jnp.where(lane == j, g, 0.0), axis=1, keepdims=True)
-        h_col = jnp.sum(jnp.where(lane == j, h, 0.0), axis=1, keepdims=True)
-        m_col = jnp.sum(jnp.where(lane == j + 64, h, 0.0), axis=1, keepdims=True)
-        pivot = jnp.sum(jnp.where(lane1 == j, g_row, 0.0), axis=1, keepdims=True)
-        entry = jnp.sum(jnp.where(lane1 == j, h_row, 0.0), axis=1, keepdims=True)
-        inv = lax.rsqrt(pivot)
-        inv = inv * (1.5 - 0.5 * pivot * inv * inv)
-        scaled = g_row * inv
-        turn = 1.0 / (entry + pivot * inv)
-        rk[at] = -scaled
-        gk[...] = g - (g_col * inv) * scaled
-        factor = jnp.where(left, h_col * turn, m_col + g_col * inv)
-        factor = jnp.where(deep > j, factor, 0.0)
-        h_line = jnp.where(left1, h_row + scaled, h_row * turn)
-        l_line = jnp.where(left1, l_row, l_row * turn)
-        lno[at] = l_line
-        hh[...] = h - factor * h_line
-        ln[...] = l - factor * l_line
-
-    loop(0, 24, column)
+        g1, g2, h1, h2, l1, l2 = gk[one], gk[two], hh[one], hh[two], ln[one], ln[two]
+        a, b, d = pick(g1, lane1, j), pick(g1, lane1, i), pick(g2, lane1, i)
+        h11, h12 = pick(h1, lane1, j), pick(h1, lane1, i)
+        h21, h22 = pick(h2, lane1, j), pick(h2, lane1, i)
+        gc1, gc2 = pick(g, lane, j), pick(g, lane, i)
+        hc1, hc2 = pick(h, lane, j), pick(h, lane, i)
+        mc1, mc2 = pick(h, lane, j + 64), pick(h, lane, i + 64)
+        inv1 = inverse_root(a)
+        s1, c1, t = g1 * inv1, gc1 * inv1, b * inv1
+        rest = d - t * t
+        inv2 = inverse_root(rest)
+        s2, c2 = (g2 - t * s1) * inv2, (gc2 - t * c1) * inv2
+        rk[one] = -s1
+        rk[two] = -s2
+        gk[...] = g - c1 * s1 - c2 * s2
+        turn1 = 1.0 / (h11 + a * inv1)
+        m12 = h12 + t
+        l21 = h21 * turn1
+        turn2 = 1.0 / (h22 - l21 * m12 + rest * inv2)
+        lc1, mr1 = hc1 * turn1, mc1 + c1
+        lc2, mr2 = (hc2 - lc1 * m12) * turn2, mc2 - mr1 * l21 + c2
+        f1 = jnp.where(deep > j, jnp.where(left, lc1, mr1), 0.0)
+        f2 = jnp.where(deep > i, jnp.where(left, lc2, mr2), 0.0)
+        f21 = jnp.where(left1, l21, m12)
+        hl1 = jnp.where(left1, h1 + s1, h1 * turn1)
+        h2 = h2 - f21 * hl1
+        hl2 = jnp.where(left1, h2 + s2, h2 * turn2)
+        ll1 = jnp.where(left1, l1, l1 * turn1)
+        l2 = l2 - f21 * ll1
+        ll2 = jnp.where(left1, l2, l2 * turn2)
+        lno[one] = ll1
+        lno[two] = ll2
+        hh[...] = h - f1 * hl1 - f2 * hl2
+        ln[...] = l - f1 * ll1 - f2 * ll2
+
+    loop(0, 12, pair)
 
     @pl.when(chip != col)
     def _():
@@ -307,8 +338,15 @@
     def _():
         pp_ref[...] = p3[col]
 
-    share(2, pp_ref)
-    loop(24, 64, column)
+    slot = core * 16 + chip
+
+    def share(d):
+        i = peer(d)
+        return remote(own3, d3.at[slot], ds_sem.at[i], dr_sem.at[chip], plane(i))
+
+    loop(1, 16, lambda d: share(d).start())
+    d3[slot] = own3[...]
+    loop(12, 32, pair)
 
     band = jnp.where(
         lax.broadcasted_iota(jnp.int32, (64, 64), 0)
@@ -320,12 +358,11 @@
 
     def wait_rows(d):
         i = peer(d)
-        for which in range(3):
-            to = d3.at[which, core * 16 + i]
-            remote(to, to, ds_sem.at[which, i], dr_sem.at[which, i], plane(i)).wait_recv()
+        to = d3.at[core * 16 + i]
+        remote(to, to, ds_sem.at[i], dr_sem.at[i], plane(i)).wait_recv()
 
     loop(1, 16, wait_rows)
-    own = d3.at[:, mine]
+    own = d3.at[mine]
     send_d = remote(own, own, one_send.at[6], one_recv.at[7], near)
     send_d.start()
 
@@ -345,7 +382,7 @@
     def _():
         wait_spread(0)
 
-    begun = mm(jnp.concatenate([from_slabs(zr, 0), from_slabs(br, 0)], axis=1), maps)
+    begun = mm(jnp.concatenate([from_slabs(lambda i: zr[i]), from_slabs(lambda i: br[i])], axis=1), maps)
     inner = mm(ys, begun, 0, 0)
 
     j_ref[...] = fold(inner)
@@ -366,17 +403,61 @@
 
     send_d.wait_recv()
     send_d.wait_send()
-    rights = []
-    for which in range(3):
-        rights.append(jnp.concatenate([from_slabs(d3.at[which], 0), from_slabs(d3.at[which], 16)], axis=0))
+    rights = [
+        jnp.concatenate(
+            [from_slabs(lambda i: d3[k * 16 + i, which]) for k in range(2)], axis=0
+        )
+        for which in range(3)
+    ]
     zero_col = (col == 0).astype(F32)
     yc = jnp.concatenate([rights[2][:WIDTH] - zero_col * band, rights[2][WIDTH:]], axis=0)
     yc_ref[...] = yc
     right = jnp.concatenate([rights[0], rights[1], yc], axis=1)
-    whole_left = jnp.concatenate([spread_left, begun], axis=1)
+    whole_left = halves(jnp.concatenate([spread_left, begun], axis=1))
     for b in range(3):
         cut = slice(256 * b, 256 * b + 256)
-        base_ref[:, cut] = a_ref[:, cut] - mm(whole_left, right[cut], 1, 1)
+        base_ref[:, cut] = a_ref[:, cut] - mm3(whole_left, halves(right[cut]))
+
+    send_gh.wait_send()
+    send_t.wait_send()
+    send_gx.wait_send()
+    send_j.wait_send()
+
+    @pl.when(chip != col)
+    def _():
+        send_pp.wait_send()
+
+    def sent(d):
+        i = peer(d)
+        remote(gs_ref.at[0], gr_ref.at[chip], gs_sem.at[i], gr_sem.at[chip], plane(i)).wait_send()
+        remote(t3.at[i], tr.at[chip], ts_sem.at[i], tr_sem.at[chip], plane(i)).wait_send()
+        share(d).wait_send()
+
+    loop(1, 16, sent)
+
+    @pl.when(chip == 0)
+    def _():
+        def head_sent(d):
+            i = peer(d)
+            remote(gs_ref.at[1], hx_ref, hs_sem.at[i], one_recv.at[5], plane(i)).wait_send()
+
+        loop(1, 16, head_sent)
+
+    @pl.when(row == 0)
+    def _():
+        loop(1, 16, lambda i: first_slab(i, 0).wait_send())
+        loop(0, 16, lambda i: first_slab(i, 1).wait_send())
+
+    def spread_sent(d):
+        z = (col + d) % 16
+        remote(zs, zr.at[chip], zs_sem.at[z], zr_sem.at[chip], swap).wait_send()
+        remote(bs, br.at[chip], ys_sem.at[z], yr_sem.at[chip], swap).wait_send()
+
+    loop(1, 16, spread_sent)
+
+    @pl.when(chip != col)
+    def _():
+        spread_sent(0)
 
     loop(1, 16, wait_inner)
     total = jr_ref[0]
@@ -386,49 +467,11 @@
     send_jx = remote(jx_ref.at[half], jx_ref.at[half], one_send.at[9], one_recv.at[9], near)
     send_jx.start()
 
-    send_gh.wait_send()
-    send_t.wait_send()
-    send_gx.wait_send()
-    send_j.wait_send()
-
-    @pl.when(chip != col)
-    def _():
-        send_pp.wait_send()
-
-    @pl.when(row == 0)
-    def _():
-        send_b.wait_send()
-
-    def sent(d):
-        i = peer(d)
-        remote(gs_ref.at[0], gr_ref.at[chip], gs_sem.at[i], gr_sem.at[chip], plane(i)).wait_send()
-        remote(t3.at[i], tr.at[chip], ts_sem.at[i], tr_sem.at[chip], plane(i)).wait_send()
+    def inner_sent(d):
+        i = peer(d)
         remote(jr_ref.at[chip], jr_ref.at[chip], js_sem.at[i], jr_sem.at[chip], plane(i)).wait_send()
-        for which in range(3):
-            remote(zs, zs, ds_sem.at[which, i], dr_sem.at[which, i], plane(i)).wait_send()
-
-    loop(1, 16, sent)
-
-    @pl.when(chip == 0)
-    def _():
-        def head_sent(d):
-            i = peer(d)
-            remote(gs_ref.at[1], hx_ref, hs_sem.at[i], one_recv.at[5], plane(i)).wait_send()
-            remote(b3.at[i], bs, bs_sem.at[i], one_recv.at[6], plane(i)).wait_send()
-
-        loop(1, 16, head_sent)
-
-    def spread_sent(d):
-        z = (col + d) % 16
-        remote(zs, zr.at[chip], zs_sem.at[z], zr_sem.at[chip], swap).wait_send()
-        remote(bs, br.at[chip], ys_sem.at[z], yr_sem.at[chip], swap).wait_send()
-
-    loop(1, 16, spread_sent)
-
-    @pl.when(chip != col)
-    def _():
-        spread_sent(0)
-
+
+    loop(1, 16, inner_sent)
     send_jx.wait_recv()
     yj_ref[...] = mm(y, unfold(jx_ref[...]))
     send_jx.wait_send()
@@ -451,8 +494,8 @@
         scratch_shapes=[
             vmem((ROWS, COLS), F32),
             vmem((WIDTH, ROWS), F32),
-            slabs(16), slabs(), slabs(32), slabs(16), slabs(16), slabs(),
-            slabs(32), slabs(), slabs(3, 32), slabs(16), slabs(16),
+            slabs(16), slabs(32), slabs(16), slabs(16), slabs(3),
+            slabs(32), slabs(32, 3), slabs(16), slabs(16),
             vmem((2, 32, 128), F32),
             vmem((2, 32, 128), F32),
             vmem((16, 16, 128), F32),
@@ -466,24 +509,32 @@
         ]
         + [vmem((64, 128), F32)] * 5
         + [dma((4,)), dma((10,)), dma((10,))]
-        + [dma((16,))] * 12
-        + [dma((3, 16))] * 2,
+        + [dma((16,))] * 5
+        + [dma((32,))]
+        + [dma((16,))] * 8,
         compiler_params=pltpu.CompilerParams(
             collective_id=0, has_side_effects=True, vmem_limit_bytes=40 * 1024 * 1024
         ),
         cost_estimate=pl.CostEstimate(flops=10**9, bytes_accessed=10**7, transcendentals=0),
-    )(matrix, panel.T)
-
-
-def update_kernel(base_ref, yj_ref, yc_ref, band_ref, out_ref, band_out):
+    )(matrix, panel)
+
+
+def update_kernel(base_ref, yj_ref, yc_ref, band_ref, out_hbm, band_out, out, done):
     band_out[...] = band_ref[...]
-    yj = yj_ref[...]
+    yc = halves(yc_ref[...])
+    copies = []
     for b in range(3):
-        cut = slice(256 * b, 256 * b + 256)
-        out_ref[:, cut] = base_ref[:, cut] + mm(yj, yc_ref[cut], 1, 1)
+        cut = slice(128 * b, 128 * b + 128)
+        out[cut] = base_ref[cut] + mm3(halves(yj_ref[cut]), yc)
+        copies.append(pltpu.make_async_copy(out.at[cut], out_hbm.at[cut], done.at[b]))
+        copies[-1].start()
+    for copy in copies:
+        copy.wait()
 
 
 def body(matrix, panel):
+    matrix = pltpu.with_memory_space_constraint(matrix, pltpu.HBM)
+    panel = pltpu.with_memory_space_constraint(panel.T, pltpu.HBM)
     band, base, yj, yc = gathered(matrix, panel)
     return pl.pallas_call(
         update_kernel,
@@ -491,6 +542,12 @@
             jax.ShapeDtypeStruct((ROWS, COLS), F32),
             jax.ShapeDtypeStruct((WIDTH, WIDTH), F32),
         ),
+        in_specs=[pl.BlockSpec(memory_space=pltpu.VMEM)] * 4,
+        out_specs=(
+            pl.BlockSpec(memory_space=pltpu.HBM),
+            pl.BlockSpec(memory_space=pltpu.VMEM),
+        ),
+        scratch_shapes=[pltpu.VMEM((ROWS, COLS), F32), pltpu.SemaphoreType.DMA((3,))],
         compiler_params=pltpu.CompilerParams(vmem_limit_bytes=40 * 1024 * 1024),
         cost_estimate=pl.CostEstimate(flops=10**8, bytes_accessed=10**7, transcendentals=0),
     )(base, yj, yc, band)

time: 55.5 us -> 50.6 us (0.912)
  Pallas kernels: 52.5 us -> 49.8 us
  local copies, waits for them, and re-layouts: 2.16 us -> 0 us
    pallas_call x1, Pallas kernels: 50.4 us -> 47.7 us  [gathered(): pl.pallas_call(gather_kernel, out_shape=(jax.ShapeDtypeStruct((WIDTH, WID...]
    unnamed x4 -> x0, local copies, waits for them, and re-layouts: 2.16 us -> none
where the time goes in v3:
time: 50.6 us; the launch traced here: 50.4 us
  Pallas kernels  49.8 us (98%)
  between operations  0.64 us (1%)
    pallas_call x1, Pallas kernels, gathered(): pl.pallas_call(gather_kernel, out_shape=(jax.ShapeDtypeStruct((WIDTH, WID...  47.7 us
    pallas_call x1, Pallas kernels, body(): pl.pallas_call(update_kernel, out_shape=(jax.ShapeDtypeStruct((ROWS, COLS...  2.13 us

profile of v3, /device:TPU:1, one launch (start us, length us, event | category | flops | bytes accessed | tf_op | source)
XLA Modules:
  0.0 50.4 jit_solution(9059179092225766699)
XLA Ops:
  0.6 47.7 %shard_map.41 = (f32[64,64]{1,0:T(8,128)S(1)}, f32[384,768]{1,0:T(8,128)S(1)}, f32[384,64]{1,0:T(8,128)S(1)}, f32[768,64]{1,0:T(8,128)S(1)}) custom-call(f32[384,768]{1,0:T(8,128)} %a_hbm.1, f32[64,384]{1,0:T(8,128)} %bitcast.1), custom_call_target="tpu_custom_call" | custom-call | flops 1000000000 | bytes 10000000 | tf_op jit(solution)/shard_map/pallas_call | solution.py:484
  48.3 2.1 %shard_map.42 = (f32[384,768]{1,0:T(8,128)}, f32[64,64]{1,0:T(8,128)}) custom-call(f32[384,768]{1,0:T(8,128)S(1)} %get-tuple-element.6.base_ref, f32[384,64]{1,0:T(8,128)S(1)} %get-tuple-element.7.yj_ref, f32[768,64]{1,0:T(8,128)S(1)} %get-tuple-element.8.yc_ref, f32[64,64]{1,0:T(8,128)S(1)} %get-tuple-element.9.band_ref), custom_call_target="tpu_custom_call" | custom-call | flops 100000000 | bytes 10000000 | tf_op jit(solution)/shard_map/pallas_call | solution.py:539

commit v4 on v3

--- a/solution.py
+++ b/solution.py
@@ -114,6 +114,15 @@
         def _():
             greet((0, col))
 
+    ring = (col + 8) % 16 - 8
+    beside = jnp.where(ring < 0, -ring, ring)
+
+    @pl.when(beside > 0)
+    def _():
+        @pl.when(beside < 3)
+        def _():
+            greet((row, 0))
+
     loads[0].wait()
     pt = pt_ref[...]
     panel = pt.T
@@ -129,25 +138,46 @@
     to_slabs(t3, 0, partial[:ROWS])
     to_slabs(t3, 16, partial[ROWS:])
 
+    @pl.when(col == 0)
+    def _():
+        to_slabs(br, 0, a_ref[:, :WIDTH])
+
+    @pl.when(row == 0)
+    def _():
+        first_columns = a_ref[:WIDTH].T
+        to_slabs(b3, 0, first_columns[:ROWS])
+        to_slabs(b3, 16, first_columns[ROWS:])
+        bs[...] = b3[0]
+
+        @pl.when(col == 0)
+        def _():
+            pl.semaphore_wait(barrier, 50)
+
+        @pl.when(col > 0)
+        def _():
+            pl.semaphore_wait(barrier, 47)
+
     @pl.when(row > 0)
     def _():
-        @pl.when(chip != col)
-        def _():
-            pl.semaphore_wait(barrier, 32)
-
-        @pl.when(chip == col)
-        def _():
-            pl.semaphore_wait(barrier, 31)
-
-    @pl.when(row == 0)
-    def _():
+        @pl.when(col == 0)
+        def _():
+            @pl.when(chip == 0)
+            def _():
+                pl.semaphore_wait(barrier, 35)
+
+            @pl.when(chip > 0)
+            def _():
+                pl.semaphore_wait(barrier, 36)
+
         @pl.when(col > 0)
         def _():
-            pl.semaphore_wait(barrier, 47)
-
-        @pl.when(col == 0)
-        def _():
-            pl.semaphore_wait(barrier, 46)
+            @pl.when(chip == col)
+            def _():
+                pl.semaphore_wait(barrier, 31)
+
+            @pl.when(chip != col)
+            def _():
+                pl.semaphore_wait(barrier, 32)
 
     send_gh = remote(gh_ref, gh1_ref, one_send.at[0], one_recv.at[0], near)
     send_gh.start()
@@ -165,14 +195,13 @@
             b3.at[k * 16 + i], bs, bs_sem.at[k * 16 + i], one_recv.at[6], (i * 2 + k, col)
         )
 
+    def first_rows_to(z):
+        return remote(br, br, ys_sem.at[z], one_recv.at[10], (row, z))
+
     @pl.when(row == 0)
     def _():
-        first_columns = a_ref[:WIDTH].T
-        to_slabs(b3, 0, first_columns[:ROWS])
-        to_slabs(b3, 16, first_columns[ROWS:])
         loop(1, 16, lambda i: first_slab(i, 0).start())
         loop(0, 16, lambda i: first_slab(i, 1).start())
-        bs[...] = b3[0]
 
     send_gh.wait_recv()
     half = pl.ds(pl.multiple_of(core * 16, 8), 16)
@@ -222,12 +251,6 @@
         @pl.when(chip == col)
         def _():
             dst[chip] = src[...]
-
-    @pl.when(row > 0)
-    def _():
-        first_slab(0, 0).wait_recv()
-
-    spread(bs, br, ys_sem, yr_sem)
 
     def wait_gram(d):
         i = peer(d)
@@ -263,6 +286,38 @@
         total = total + tr[i]
     zs[...] = total
     spread(zs, zr, zs_sem, zr_sem)
+
+    @pl.when(col == 0)
+    def _():
+        for z in (1, 15, 2, 14):
+            first_rows_to(z).start()
+
+    @pl.when(row > 0)
+    def _():
+        first_slab(0, 0).wait_recv()
+
+    def first_to(d):
+        z = 3 + (col + d) % 11
+        return z, remote(bs, br.at[chip], ys_sem.at[z], yr_sem.at[chip], (col * 2 + core, z))
+
+    def send_first(d):
+        z, copy = first_to(d)
+
+        @pl.when(chip != col)
+        def _():
+            copy.start()
+
+        @pl.when(chip == col)
+        def _():
+            @pl.when(z != col)
+            def _():
+                copy.start()
+
+            @pl.when(z == col)
+            def _():
+                br[chip] = bs[...]
+
+    loop(0, 11, send_first)
 
     send_gx.wait_recv()
     gram = unfold(gx_ref[0])
@@ -369,12 +424,43 @@
     y = jnp.concatenate([panel[:WIDTH] - is_first * band, panel[WIDTH:]], axis=0)
     ys = mm(y, s)
     spread_left = jnp.concatenate([mm(y, s, 1, 1), -mm(y, rs, 1, 1)], axis=1)
-    maps = jnp.concatenate([s, -rs], axis=0)
+    folded_ys = fold(ys)
+
+    def twice(block):
+        none = jnp.zeros_like(block)
+        return jnp.concatenate(
+            [jnp.concatenate([block, none], axis=1), jnp.concatenate([none, block], axis=1)],
+            axis=0,
+        )
+
+    def stacked(ref):
+        return jnp.concatenate([ref[i] for i in range(16)], axis=0)
+
+    twice_s = twice(s)
+
+    @pl.when(beside > 0)
+    def _():
+        @pl.when(beside < 3)
+        def _():
+            first_rows_to(0).wait_recv()
+
+    @pl.when(beside > 2)
+    def _():
+        def wait_first(d):
+            i = peer(d)
+            remote(bs, br.at[i], ys_sem.at[i], yr_sem.at[i], swap).wait_recv()
+
+        loop(1, 16, wait_first)
+
+        @pl.when(chip != col)
+        def _():
+            wait_first(0)
+
+    first_part = mm(stacked(br), twice(rs))
 
     def wait_spread(d):
         i = peer(d)
         remote(zs, zr.at[i], zs_sem.at[i], zr_sem.at[i], swap).wait_recv()
-        remote(bs, br.at[i], ys_sem.at[i], yr_sem.at[i], swap).wait_recv()
 
     loop(1, 16, wait_spread)
 
@@ -382,8 +468,9 @@
     def _():
         wait_spread(0)
 
-    begun = mm(jnp.concatenate([from_slabs(lambda i: zr[i]), from_slabs(lambda i: br[i])], axis=1), maps)
-    inner = mm(ys, begun, 0, 0)
+    folded_begun = mm(stacked(zr), twice_s) - first_part
+    inner = mm(folded_ys, folded_begun, 0, 0)
+    inner = inner[:64, :64] + inner[64:, 64:]
 
     j_ref[...] = fold(inner)
     send_j = remote(j_ref, j1_ref, one_send.at[8], one_recv.at[8], near)
@@ -413,6 +500,7 @@
     yc = jnp.concatenate([rights[2][:WIDTH] - zero_col * band, rights[2][WIDTH:]], axis=0)
     yc_ref[...] = yc
     right = jnp.concatenate([rights[0], rights[1], yc], axis=1)
+    begun = unfold(folded_begun)
     whole_left = halves(jnp.concatenate([spread_left, begun], axis=1))
     for b in range(3):
         cut = slice(256 * b, 256 * b + 256)
@@ -448,10 +536,29 @@
         loop(1, 16, lambda i: first_slab(i, 0).wait_send())
         loop(0, 16, lambda i: first_slab(i, 1).wait_send())
 
+    @pl.when(col == 0)
+    def _():
+        for z in (1, 15, 2, 14):
+            first_rows_to(z).wait_send()
+
+    def first_sent(d):
+        z, copy = first_to(d)
+
+        @pl.when(chip != col)
+        def _():
+            copy.wait_send()
+
+        @pl.when(chip == col)
+        def _():
+            @pl.when(z != col)
+            def _():
+                copy.wait_send()
+
+    loop(0, 11, first_sent)
+
     def spread_sent(d):
         z = (col + d) % 16
         remote(zs, zr.at[chip], zs_sem.at[z], zr_sem.at[chip], swap).wait_send()
-        remote(bs, br.at[chip], ys_sem.at[z], yr_sem.at[chip], swap).wait_send()
 
     loop(1, 16, spread_sent)
 
@@ -508,7 +615,7 @@
             vmem((32, 128), F32),
         ]
         + [vmem((64, 128), F32)] * 5
-        + [dma((4,)), dma((10,)), dma((10,))]
+        + [dma((4,)), dma((10,)), dma((11,))]
         + [dma((16,))] * 5
         + [dma((32,))]
         + [dma((16,))] * 8,

time: 50.6 us -> 49.3 us (0.974)
  Pallas kernels: 49.8 us -> 48.6 us
    pallas_call x1, Pallas kernels: 47.7 us -> 46.4 us  [gathered(): pl.pallas_call(gather_kernel, out_shape=(jax.ShapeDtypeStruct((WIDTH, WID...]
where the time goes in v4:
time: 49.3 us; the launch traced here: 49.2 us
  Pallas kernels  48.6 us (99%)
  between operations  0.64 us (1%)
    pallas_call x1, Pallas kernels, gathered(): pl.pallas_call(gather_kernel, out_shape=(jax.ShapeDtypeStruct((WIDTH, WID...  46.4 us
    pallas_call x1, Pallas kernels, body(): pl.pallas_call(update_kernel, out_shape=(jax.ShapeDtypeStruct((ROWS, COLS...  2.13 us

profile of v4, /device:TPU:1, one launch (start us, length us, event | category | flops | bytes accessed | tf_op | source)
XLA Modules:
  0.0 49.2 jit_solution(15851007773996967614)
XLA Ops:
  0.6 46.4 %shard_map.41 = (f32[64,64]{1,0:T(8,128)S(1)}, f32[384,768]{1,0:T(8,128)S(1)}, f32[384,64]{1,0:T(8,128)S(1)}, f32[768,64]{1,0:T(8,128)S(1)}) custom-call(f32[384,768]{1,0:T(8,128)} %a_hbm.1, f32[64,384]{1,0:T(8,128)} %bitcast.1), custom_call_target="tpu_custom_call" | custom-call | flops 1000000000 | bytes 10000000 | tf_op jit(solution)/shard_map/pallas_call | solution.py:591
  47.1 2.1 %shard_map.42 = (f32[384,768]{1,0:T(8,128)}, f32[64,64]{1,0:T(8,128)}) custom-call(f32[384,768]{1,0:T(8,128)S(1)} %get-tuple-element.6.base_ref, f32[384,64]{1,0:T(8,128)S(1)} %get-tuple-element.7.yj_ref, f32[768,64]{1,0:T(8,128)S(1)} %get-tuple-element.8.yc_ref, f32[64,64]{1,0:T(8,128)S(1)} %get-tuple-element.9.band_ref), custom_call_target="tpu_custom_call" | custom-call | flops 100000000 | bytes 10000000 | tf_op jit(solution)/shard_map/pallas_call | solution.py:646

commit v5 on v4

--- a/solution.py
+++ b/solution.py
@@ -58,7 +58,7 @@
     a_hbm, p_hbm, band_ref, base_ref, yj_ref, yc_ref,
     a_ref, pt_ref, p3, t3, t1, tr, own3, b3, d3, zr, br,
     gh_ref, gh1_ref, gr_ref, gx_ref, hx_ref, gs_ref,
-    j_ref, j1_ref, jr_ref, jx_ref,
+    j_ref, j1_ref, jr_ref,
     gk, hh, ln, rk, lno,
     load_sem, one_send, one_recv,
     gs_sem, gr_sem, hs_sem, ts_sem, tr_sem, bs_sem,
@@ -119,7 +119,7 @@
 
     @pl.when(beside > 0)
     def _():
-        @pl.when(beside < 3)
+        @pl.when(beside < 4)
         def _():
             greet((row, 0))
 
@@ -151,7 +151,7 @@
 
         @pl.when(col == 0)
         def _():
-            pl.semaphore_wait(barrier, 50)
+            pl.semaphore_wait(barrier, 52)
 
         @pl.when(col > 0)
         def _():
@@ -163,11 +163,11 @@
         def _():
             @pl.when(chip == 0)
             def _():
-                pl.semaphore_wait(barrier, 35)
+                pl.semaphore_wait(barrier, 37)
 
             @pl.when(chip > 0)
             def _():
-                pl.semaphore_wait(barrier, 36)
+                pl.semaphore_wait(barrier, 38)
 
         @pl.when(col > 0)
         def _():
@@ -179,10 +179,10 @@
             def _():
                 pl.semaphore_wait(barrier, 32)
 
+    send_t = remote(t3.at[pl.ds(other * 16, 16)], t1, one_send.at[2], one_recv.at[2], near)
+    send_t.start()
     send_gh = remote(gh_ref, gh1_ref, one_send.at[0], one_recv.at[0], near)
     send_gh.start()
-    send_t = remote(t3.at[pl.ds(other * 16, 16)], t1, one_send.at[2], one_recv.at[2], near)
-    send_t.start()
 
     send_pp = remote(p3.at[col], pp_ref, one_send.at[1], one_recv.at[1], swap)
 
@@ -198,10 +198,17 @@
     def first_rows_to(z):
         return remote(br, br, ys_sem.at[z], one_recv.at[10], (row, z))
 
-    @pl.when(row == 0)
-    def _():
-        loop(1, 16, lambda i: first_slab(i, 0).start())
-        loop(0, 16, lambda i: first_slab(i, 1).start())
+
+    send_t.wait_recv()
+    mine = pl.ds(core * 16, 16)
+    t3[mine] = t3[mine] + t1[...]
+
+    def send_part(d):
+        i = peer(d)
+        remote(t3.at[core * 16 + i], tr.at[chip], ts_sem.at[i], tr_sem.at[chip], plane(i)).start()
+
+    loop(1, 16, send_part)
+    tr[chip] = t3[core * 16 + chip]
 
     send_gh.wait_recv()
     half = pl.ds(pl.multiple_of(core * 16, 8), 16)
@@ -218,22 +225,18 @@
 
     loop(1, 16, send_gram)
 
+
+    gr_ref[chip] = gs_ref[0]
+
+
     @pl.when(chip == 0)
     def _():
         loop(1, 16, send_head)
 
-    gr_ref[chip] = gs_ref[0]
-
-    send_t.wait_recv()
-    mine = pl.ds(core * 16, 16)
-    t3[mine] = t3[mine] + t1[...]
-
-    def send_part(d):
-        i = peer(d)
-        remote(t3.at[core * 16 + i], tr.at[chip], ts_sem.at[i], tr_sem.at[chip], plane(i)).start()
-
-    loop(1, 16, send_part)
-    tr[chip] = t3[core * 16 + chip]
+    @pl.when(row == 0)
+    def _():
+        loop(1, 16, lambda i: first_slab(i, 0).start())
+        loop(0, 16, lambda i: first_slab(i, 1).start())
 
     slot = core * 16 + chip
 
@@ -251,6 +254,17 @@
         @pl.when(chip == col)
         def _():
             dst[chip] = src[...]
+
+    def wait_part(d):
+        i = peer(d)
+        remote(t3.at[core * 16 + i], tr.at[i], ts_sem.at[i], tr_sem.at[i], plane(i)).wait_recv()
+
+    loop(1, 16, wait_part)
+    total = tr[0]
+    for i in range(1, 16):
+        total = total + tr[i]
+    zs[...] = total
+    spread(zs, zr, zs_sem, zr_sem)
 
     def wait_gram(d):
         i = peer(d)
@@ -276,20 +290,10 @@
     )
     send_gx.start()
 
-    def wait_part(d):
-        i = peer(d)
-        remote(t3.at[core * 16 + i], tr.at[i], ts_sem.at[i], tr_sem.at[i], plane(i)).wait_recv()
-
-    loop(1, 16, wait_part)
-    total = tr[0]
-    for i in range(1, 16):
-        total = total + tr[i]
-    zs[...] = total
-    spread(zs, zr, zs_sem, zr_sem)
 
     @pl.when(col == 0)
     def _():
-        for z in (1, 15, 2, 14):
+        for z in (1, 15, 2, 14, 3, 13):
             first_rows_to(z).start()
 
     @pl.when(row > 0)
@@ -297,7 +301,7 @@
         first_slab(0, 0).wait_recv()
 
     def first_to(d):
-        z = 3 + (col + d) % 11
+        z = 4 + (col + d) % 9
         return z, remote(bs, br.at[chip], ys_sem.at[z], yr_sem.at[chip], (col * 2 + core, z))
 
     def send_first(d):
@@ -317,7 +321,7 @@
             def _():
                 br[chip] = bs[...]
 
-    loop(0, 11, send_first)
+    loop(0, 9, send_first)
 
     send_gx.wait_recv()
     gram = unfold(gx_ref[0])
@@ -440,11 +444,11 @@
 
     @pl.when(beside > 0)
     def _():
-        @pl.when(beside < 3)
+        @pl.when(beside < 4)
         def _():
             first_rows_to(0).wait_recv()
 
-    @pl.when(beside > 2)
+    @pl.when(beside > 3)
     def _():
         def wait_first(d):
             i = peer(d)
@@ -472,11 +476,18 @@
     inner = mm(folded_ys, folded_begun, 0, 0)
     inner = inner[:64, :64] + inner[64:, 64:]
 
-    j_ref[...] = fold(inner)
+    at_row = lax.broadcasted_iota(jnp.int32, (32, 32), 0)
+    at_lane = lax.broadcasted_iota(jnp.int32, (32, 32), 1)
+    inner = 0.5 * (inner + inner.T)
+    corner = inner[32:, 32:]
+    mixed = jnp.where(at_row <= at_lane, inner[:32, :32], corner)
+    j_ref[:16] = fold(jnp.concatenate([mixed, inner[:32, 32:]], axis=1))
+    j_ref[16:, :32] = jnp.sum(jnp.where(at_row == at_lane, corner, 0.0), axis=0, keepdims=True)
+    j_ref[16:, 32:] = jnp.zeros((1, 96), F32)
     send_j = remote(j_ref, j1_ref, one_send.at[8], one_recv.at[8], near)
     send_j.start()
     send_j.wait_recv()
-    jr_ref[chip] = j_ref[half] + j1_ref[half]
+    jr_ref[chip] = j_ref[...] + j1_ref[...]
 
     def send_inner(d):
         i = peer(d)
@@ -538,7 +549,7 @@
 
     @pl.when(col == 0)
     def _():
-        for z in (1, 15, 2, 14):
+        for z in (1, 15, 2, 14, 3, 13):
             first_rows_to(z).wait_send()
 
     def first_sent(d):
@@ -554,7 +565,7 @@
             def _():
                 copy.wait_send()
 
-    loop(0, 11, first_sent)
+    loop(0, 9, first_sent)
 
     def spread_sent(d):
         z = (col + d) % 16
@@ -570,18 +581,25 @@
     total = jr_ref[0]
     for i in range(1, 16):
         total = total + jr_ref[i]
-    jx_ref[half] = total
-    send_jx = remote(jx_ref.at[half], jx_ref.at[half], one_send.at[9], one_recv.at[9], near)
-    send_jx.start()
-
     def inner_sent(d):
         i = peer(d)
         remote(jr_ref.at[chip], jr_ref.at[chip], js_sem.at[i], jr_sem.at[chip], plane(i)).wait_send()
 
     loop(1, 16, inner_sent)
-    send_jx.wait_recv()
-    yj_ref[...] = mm(y, unfold(jx_ref[...]))
-    send_jx.wait_send()
+    packed = unfold(total[:16])
+    mixed, side = packed[:, :32], packed[:, 32:]
+    upper = jnp.where(at_row <= at_lane, mixed, 0.0)
+    lower = jnp.where(at_row > at_lane, mixed, 0.0)
+    strict = jnp.where(at_row < at_lane, mixed, 0.0)
+    corner = lower + lower.T + jnp.where(at_row == at_lane, total[16:, :32], 0.0)
+    coupling = jnp.concatenate(
+        [
+            jnp.concatenate([upper + strict.T, side], axis=1),
+            jnp.concatenate([side.T, corner], axis=1),
+        ],
+        axis=0,
+    )
+    yj_ref[...] = mm(y, coupling)
 
 
 def gathered(matrix, panel):
@@ -609,10 +627,9 @@
             vmem((2, 32, 128), F32),
             vmem((16, 128), F32),
             vmem((2, 16, 128), F32),
-            vmem((32, 128), F32),
-            vmem((32, 128), F32),
-            vmem((16, 16, 128), F32),
-            vmem((32, 128), F32),
+            vmem((17, 128), F32),
+            vmem((17, 128), F32),
+            vmem((16, 17, 128), F32),
         ]
         + [vmem((64, 128), F32)] * 5
         + [dma((4,)), dma((10,)), dma((11,))]
@@ -628,12 +645,12 @@
 
 def update_kernel(base_ref, yj_ref, yc_ref, band_ref, out_hbm, band_out, out, done):
     band_out[...] = band_ref[...]
-    yc = halves(yc_ref[...])
+    yj = halves(yj_ref[...])
     copies = []
     for b in range(3):
-        cut = slice(128 * b, 128 * b + 128)
-        out[cut] = base_ref[cut] + mm3(halves(yj_ref[cut]), yc)
-        copies.append(pltpu.make_async_copy(out.at[cut], out_hbm.at[cut], done.at[b]))
+        cut = pl.ds(256 * b, 256)
+        out[:, cut] = base_ref[:, cut] + mm3(yj, halves(yc_ref[cut]))
+        copies.append(pltpu.make_async_copy(out.at[:, cut], out_hbm.at[:, cut], done.at[b]))
         copies[-1].start()
     for copy in copies:
         copy.wait()

time: 49.3 us -> 48.6 us (0.986)
  Pallas kernels: 48.6 us -> 47.8 us
    pallas_call x1, Pallas kernels: 46.4 us -> 45.7 us  [gathered(): pl.pallas_call(gather_kernel, out_shape=(jax.ShapeDtypeStruct((WIDTH, WID...]
where the time goes in v5:
time: 48.6 us; the launch traced here: 48.5 us
  Pallas kernels  47.8 us (98%)
  between operations  0.64 us (1%)
    pallas_call x1, Pallas kernels, gathered(): pl.pallas_call(gather_kernel, out_shape=(jax.ShapeDtypeStruct((WIDTH, WID...  45.7 us
    pallas_call x1, Pallas kernels, body(): pl.pallas_call(update_kernel, out_shape=(jax.ShapeDtypeStruct((ROWS, COLS...  2.16 us

profile of v5, /device:TPU:1, one launch (start us, length us, event | category | flops | bytes accessed | tf_op | source)
XLA Modules:
  0.0 48.5 jit_solution(17979923031454102232)
XLA Ops:
  0.6 45.7 %shard_map.41 = (f32[64,64]{1,0:T(8,128)S(1)}, f32[384,768]{1,0:T(8,128)S(1)}, f32[384,64]{1,0:T(8,128)S(1)}, f32[768,64]{1,0:T(8,128)S(1)}) custom-call(f32[384,768]{1,0:T(8,128)} %a_hbm.1, f32[64,384]{1,0:T(8,128)} %bitcast.1), custom_call_target="tpu_custom_call" | custom-call | flops 1000000000 | bytes 10000000 | tf_op jit(solution)/shard_map/pallas_call | solution.py:609
  46.3 2.2 %shard_map.42 = (f32[384,768]{1,0:T(8,128)}, f32[64,64]{1,0:T(8,128)}) custom-call(f32[384,768]{1,0:T(8,128)S(1)} %get-tuple-element.6.base_ref, f32[384,64]{1,0:T(8,128)S(1)} %get-tuple-element.7.yj_ref, f32[768,64]{1,0:T(8,128)S(1)} %get-tuple-element.8.yc_ref, f32[64,64]{1,0:T(8,128)S(1)} %get-tuple-element.9.band_ref), custom_call_target="tpu_custom_call" | custom-call | flops 100000000 | bytes 10000000 | tf_op jit(solution)/shard_map/pallas_call | solution.py:663

commit v6 on v5

--- a/solution.py
+++ b/solution.py
@@ -420,10 +420,6 @@
         to = d3.at[core * 16 + i]
         remote(to, to, ds_sem.at[i], dr_sem.at[i], plane(i)).wait_recv()
 
-    loop(1, 16, wait_rows)
-    own = d3.at[mine]
-    send_d = remote(own, own, one_send.at[6], one_recv.at[7], near)
-    send_d.start()
 
     y = jnp.concatenate([panel[:WIDTH] - is_first * band, panel[WIDTH:]], axis=0)
     ys = mm(y, s)
@@ -486,6 +482,10 @@
     j_ref[16:, 32:] = jnp.zeros((1, 96), F32)
     send_j = remote(j_ref, j1_ref, one_send.at[8], one_recv.at[8], near)
     send_j.start()
+    loop(1, 16, wait_rows)
+    own = d3.at[mine]
+    send_d = remote(own, own, one_send.at[6], one_recv.at[7], near)
+    send_d.start()
     send_j.wait_recv()
     jr_ref[chip] = j_ref[...] + j1_ref[...]
 
@@ -599,7 +599,7 @@
         ],
         axis=0,
     )
-    yj_ref[...] = mm(y, coupling)
+    yj_ref[...] = mm3(halves(y), halves(coupling))
 
 
 def gathered(matrix, panel):

time: 48.6 us -> 47.9 us (0.986)
  the two profiles are of different devices: /device:TPU:1 before, /device:TPU:96 now
where the time goes in v6:
time: 47.9 us; the launch traced here: 47.8 us
  Pallas kernels  47.1 us (98%)
  between operations  0.64 us (1%)
    pallas_call x1, Pallas kernels, gathered(): pl.pallas_call(gather_kernel, out_shape=(jax.ShapeDtypeStruct((WIDTH, WID...  45 us
    pallas_call x1, Pallas kernels, body(): pl.pallas_call(update_kernel, out_shape=(jax.ShapeDtypeStruct((ROWS, COLS...  2.16 us

profile of v6, /device:TPU:96, one launch (start us, length us, event | category | flops | bytes accessed | tf_op | source)
XLA Modules:
  0.0 47.8 jit_solution(9960749715578002013)
XLA Ops:
  0.6 45.0 %shard_map.41 = (f32[64,64]{1,0:T(8,128)S(1)}, f32[384,768]{1,0:T(8,128)S(1)}, f32[384,64]{1,0:T(8,128)S(1)}, f32[768,64]{1,0:T(8,128)S(1)}) custom-call(f32[384,768]{1,0:T(8,128)} %a_hbm.1, f32[64,384]{1,0:T(8,128)} %bitcast.1), custom_call_target="tpu_custom_call" | custom-call | flops 1000000000 | bytes 10000000 | tf_op jit(solution)/shard_map/pallas_call | solution.py:609
  45.6 2.2 %shard_map.42 = (f32[384,768]{1,0:T(8,128)}, f32[64,64]{1,0:T(8,128)}) custom-call(f32[384,768]{1,0:T(8,128)S(1)} %get-tuple-element.6.base_ref, f32[384,64]{1,0:T(8,128)S(1)} %get-tuple-element.7.yj_ref, f32[768,64]{1,0:T(8,128)S(1)} %get-tuple-element.8.yc_ref, f32[64,64]{1,0:T(8,128)S(1)} %get-tuple-element.9.band_ref), custom_call_target="tpu_custom_call" | custom-call | flops 100000000 | bytes 10000000 | tf_op jit(solution)/shard_map/pallas_call | solution.py:663

commit v7 on v6

--- a/solution.py
+++ b/solution.py
@@ -32,7 +32,8 @@
 
 
 def loop(lo, hi, step):
-    lax.fori_loop(lo, hi, lambda i, carry: (step(i), carry)[1], 0)
+    unroll = 5 if hi - lo == 15 else 1
+    lax.fori_loop(lo, hi, lambda i, carry: (step(i), carry)[1], 0, unroll=unroll)
 
 
 def fold(block):

time: 47.9 us -> 47.8 us (level)
  no operation moved by 1% of the time
where the time goes in v7:
time: 47.8 us; the launch traced here: 47.6 us
  Pallas kernels  47 us (98%)
  between operations  0.64 us (1%)
    pallas_call x1, Pallas kernels, gathered(): pl.pallas_call(gather_kernel, out_shape=(jax.ShapeDtypeStruct((WIDTH, WID...  44.8 us
    pallas_call x1, Pallas kernels, body(): pl.pallas_call(update_kernel, out_shape=(jax.ShapeDtypeStruct((ROWS, COLS...  2.16 us

profile of v7, /device:TPU:96, one launch (start us, length us, event | category | flops | bytes accessed | tf_op | source)
XLA Modules:
  0.0 47.6 jit_solution(5838996703392235510)
XLA Ops:
  0.6 44.8 %shard_map.41 = (f32[64,64]{1,0:T(8,128)S(1)}, f32[384,768]{1,0:T(8,128)S(1)}, f32[384,64]{1,0:T(8,128)S(1)}, f32[768,64]{1,0:T(8,128)S(1)}) custom-call(f32[384,768]{1,0:T(8,128)} %a_hbm.1, f32[64,384]{1,0:T(8,128)} %bitcast.1), custom_call_target="tpu_custom_call" | custom-call | flops 1000000000 | bytes 10000000 | tf_op jit(solution)/shard_map/pallas_call | solution.py:610
  45.5 2.2 %shard_map.42 = (f32[384,768]{1,0:T(8,128)}, f32[64,64]{1,0:T(8,128)}) custom-call(f32[384,768]{1,0:T(8,128)S(1)} %get-tuple-element.6.base_ref, f32[384,64]{1,0:T(8,128)S(1)} %get-tuple-element.7.yj_ref, f32[768,64]{1,0:T(8,128)S(1)} %get-tuple-element.8.yc_ref, f32[64,64]{1,0:T(8,128)S(1)} %get-tuple-element.9.band_ref), custom_call_target="tpu_custom_call" | custom-call | flops 100000000 | bytes 10000000 | tf_op jit(solution)/shard_map/pallas_call | solution.py:664
